TPU v7x, 128 devices: a whole 4x4x4 slice. The times are simulated.
128 devices in a mesh: ctx: 16 (over x_hi, z, core), tp: 8 (over y, x_lo).
Axes of the slice: x: 4 (x_hi: 2, x_lo: 2; x = x_hi * 2 + x_lo), y: 4, z: 4, core: 2. Of those that a mesh axis runs over, the one named last changes fastest.
Arguments:
- features: bfloat16 [16384, 3, 8192], P('ctx', None, 'tp'), may hold values from -6 to 6
- contig_starts: int32 [128], P('ctx'), may hold values 0 or 1
- short_filter: float32 [7, 3, 8192], P(None, None, 'tp'), may hold values from -2.4 to 2.4
- medium_filter: float32 [512, 128], P('tp'), may hold values from -0.54 to 0.54
- filter_bias: float32 [8192], P('tp'), may hold values from -4 to 4
- out_weight: bfloat16 [8192, 8192], P('tp', 'ctx'), may hold values from -0.0625 to 0.0625
Outputs:
- mixed: bfloat16 [16384, 8192], P('ctx', 'tp')
All inputs are finite; a program needn't handle non-finite values. No bound on the sum of `contig_starts` on one device may be relied on, other than what follows from the above.
Results may differ from a plain program's by a relative error of at most 0.017.
Values may be sent and summed in bfloat16 or wider, within the bound.
A program may use at most 128 MiB of HBM per device.

v0:
```python
import jax
import jax.numpy as jnp
from jax import lax
from jax.sharding import PartitionSpec as P

GROUP_CH = 16


def shifted(x, axis, by):
    count = lax.axis_size(axis)
    pairs = [(i, i + by) for i in range(count) if 0 <= i + by < count]
    return lax.ppermute(x, axis, pairs)


def short_conv(ext, weights, block):
    span = weights.shape[0]
    total = weights[0] * ext[:, span - 1 : span - 1 + block]
    for lag in range(1, span):
        total = total + weights[lag] * ext[:, span - 1 - lag : span - 1 - lag + block]
    return total


def toeplitz(taps):
    width = taps.shape[1]
    rows = lax.broadcasted_iota(jnp.int32, (width, width), 0)
    cols = lax.broadcasted_iota(jnp.int32, (width, width), 1)
    lag = rows - cols
    zero = jnp.zeros((), taps.dtype)
    near = jnp.where(lag >= 0, taps[:, jnp.clip(lag, 0, width - 1)], zero)
    far = jnp.where(lag < 0, taps[:, jnp.clip(lag + width, 0, width - 1)], zero)
    return (near, far)


def on_device(features, contig_starts, short_filter, medium_filter, filter_bias, out_weight):
    tok_rows, _, chans = features.shape
    span = short_filter.shape[0]
    block = medium_filter.shape[1]
    nblk = tok_rows // block
    keep = (1 - contig_starts).astype(jnp.float32)
    blocks = features.reshape(nblk, block, 3, chans)
    last_before = blocks[-2:-1, block - (span - 1) :].astype(jnp.float32) * keep[-1]
    last_ext = jnp.concatenate([last_before, blocks[-1:].astype(jnp.float32)], axis=1)
    last_filt = short_conv(last_ext, short_filter, block)
    last_gated = (last_filt[0, :, 1] * last_filt[0, :, 2]).astype(jnp.bfloat16)
    rim_rows, rim_gated = shifted((blocks[-1, block - (span - 1) :], last_gated), "ctx", 1)
    before = jnp.concatenate([rim_rows[None], blocks[:-1, block - (span - 1) :]], axis=0).astype(
        jnp.float32
    )
    before = before * keep[:, None, None, None]
    ext = jnp.concatenate([before, blocks.astype(jnp.float32)], axis=1)
    filtered = short_conv(ext, short_filter, block)
    gated = (filtered[:, :, 1] * filtered[:, :, 2]).astype(jnp.bfloat16)
    near, far = toeplitz(medium_filter.astype(jnp.bfloat16))
    groups = chans // GROUP_CH
    grouped = gated.reshape(nblk, block, groups, GROUP_CH)
    earlier = jnp.concatenate([rim_gated.reshape(1, block, groups, GROUP_CH), grouped[:-1]], axis=0)
    earlier = (earlier.astype(jnp.float32) * keep[:, None, None, None]).astype(jnp.bfloat16)
    conv = jnp.einsum("gij,bjgc->bigc", near, grouped, preferred_element_type=jnp.float32)
    conv = conv + jnp.einsum("gij,bjgc->bigc", far, earlier, preferred_element_type=jnp.float32)
    conv = conv.reshape(nblk, block, chans)
    mixer = (filtered[:, :, 0] * (conv + filter_bias * gated.astype(jnp.float32))).astype(
        jnp.bfloat16
    )
    mixer = mixer.reshape(tok_rows, chans)
    terms = jnp.dot(
        mixer,
        lax.all_gather(out_weight, "ctx", axis=1, tiled=True),
        preferred_element_type=jnp.float32,
    )
    return lax.psum_scatter(terms.astype(jnp.bfloat16), "tp", scatter_dimension=1, tiled=True)


def solution(mesh):
    in_specs = (
        P("ctx", None, "tp"),
        P("ctx"),
        P(None, None, "tp"),
        P("tp", None),
        P("tp"),
        P("tp", "ctx"),
    )
    out_specs = P("ctx", "tp")
    return jax.shard_map(
        on_device, mesh=mesh, in_specs=in_specs, out_specs=out_specs, check_vma=False
    )
```

profile of v0, /device:TPU:16, one launch (start us, length us, event | category | flops | bytes accessed | tf_op | source)
XLA Modules:
  0.0 608.2 jit_solution(13106131654786731880)
XLA Ops:
  6.5 0.0 all-gather.2.cloned.1.call-start
  6.5 0.7 all-gather.2.cloned.1.call-update
  7.3 0.0 reduce-scatter.2.cloned.1.call-start
  7.3 0.8 slice_bitcast_fusion
  8.1 1.7 collective-permute-start
  9.9 0.0 slice-start
  9.9 2.2 slice.120
  12.1 1.5 fusion.61
  13.6 0.7 subtract_convert_fusion
  14.3 0.6 slice.122
  14.9 1.5 convert_multiply_fusion.2
  16.3 1.6 copy.19
  18.0 1.5 copy.36
  19.5 0.0 slice-start.1
  19.5 0.1 convert_bitcast_fusion
  19.7 11.3 %fusion.37 = f32[1,128,3,1024]{1,3,2,0:T(8,128)S(1)} fusion(bf16[128,3,1024]{0,2,1:T(8,128)(2,1)S(1)} %copy.36, f32[1,6,3,1024]{1,3,2,0:T(8,128)} %copy.19, f32[1,128,3,1024]{1,3,2,0:T(8,128)S(1)} %convert_bitcast_fusion, f32[3,1024]{1,0:T(4,128)S(1)} %get-tuple-element.14, f32[3,1024]{1,0:T(4,128)S(1)} %get-tuple-element.15, ...), kind=kLoop, calls=%fused_computation.65 | loop fusion | flops 7864320 | bytes 4091904 | tf_op jit(solution)/shard_map/add | solution.py:19
  31.0 0.1 fusion.52
  31.1 4.5 collective-permute-start.1
  35.7 0.0 slice-done
  35.7 0.0 slice-done.1
  35.7 0.1 slice.138
  35.8 0.0 copy-start.3
  35.8 6.1 convert_element_type.57
  41.9 0.0 copy-done.3
  41.9 0.1 copy.15
  42.0 57.4 %gather_fusion = bf16[16384,64]{1,0:T(8,128)(2,1)} fusion(bf16[64,128]{0,1:T(8,128)(2,1)S(1)} %copy.15, s32[16384]{0:T(1024)S(1)} %fusion.54), kind=kCustom, calls=%fused_computation | custom fusion | bytes 4259840 | tf_op jit(solution)/shard_map/gather | solution.py:29
  99.4 5.7 copy.16
  105.0 57.4 %gather_fusion.1 = bf16[16384,64]{1,0:T(8,128)(2,1)} fusion(bf16[64,128]{0,1:T(8,128)(2,1)S(1)} %copy.15, s32[16384]{0:T(1024)S(1)} %fusion.56), kind=kCustom, calls=%fused_computation.1 | custom fusion | bytes 4259840 | tf_op jit(solution)/shard_map/gather | solution.py:30
  162.4 5.6 copy.21
  168.1 0.0 collective-permute-done
  168.1 0.1 convert_multiply_fusion.1
  168.2 35.1 %fusion.3 = f32[8,128,3,1024]{3,1,0,2:T(8,128)} fusion(f32[8,6,3,1024]{3,1,0,2:T(8,128)S(1)} %convert_multiply_fusion.1, f32[8,128,3,1024]{3,1,0,2:T(8,128)} %convert_element_type.57, f32[3,1024]{1,0:T(4,128)S(1)} %get-tuple-element.14, f32[3,1024]{1,0:T(4,128)S(1)} %get-tuple-element.15, f32[3,1024]{1,0:T(4,128)S(1)} %get-tuple-element.16, ...), kind=kLoop, calls=%fused_computation.11 | loop fusion | flops 59768832 | bytes 25841664 | tf_op jit(solution)/shard_map/add | solution.py:19
  203.4 8.0 %fusion.19 = (bf16[8,128,1,1024]{3,1,0,2:T(8,128)(2,1)S(1)}, f32[8,128,1,1024]{3,1,0,2:T(8,128)}) fusion(f32[8,128,3,1024]{3,1,0,2:T(8,128)} %fusion.3), kind=kLoop, calls=%fused_computation.43 | loop fusion | flops 2097152 | bytes 18874368 | tf_op jit(solution)/shard_map/convert_element_type | solution.py:52
  211.4 2.4 copy.14
  213.7 1.4 slice.165
  215.1 3.8 copy.20
  218.9 2.6 bitcast_convert_fusion
  221.5 5.4 copy.24
  226.9 5.6 copy.25
  232.5 0.0 copy-done.1
  232.5 3.3 fusion.22
  235.8 0.0 collective-permute-done.1
  235.8 1.6 add_bitcast_fusion
  237.4 0.0 copy-start.4
  237.5 3.9 copy.23
  241.3 31.7 %convolution_convert_fusion = bf16[1024,8192]{1,0:T(8,128)(2,1)} fusion(bf16[1024,8192]{1,0:T(8,128)(2,1)} %all-gather.2.cloned.1.call-done, f32[1024,1024]{0,1:T(8,128)} %copy.25, f32[128,8,8,128]{3,2,1,0:T(8,128)} %bitcast.96, f32[1024,1024]{0,1:T(8,128)} %copy.24, f32[1024]{0:T(1024)S(1)} %copy-done.4), kind=kOutput, calls=%fused_computation.7 | convolution fusion | flops 17192452096 | bytes 46141440 | tf_op jit(solution)/shard_map/dot_general | solution.py:65
  273.0 0.0 reduce-scatter.2.cloned.1.call-update
  273.1 328.2 %reduce-scatter.2.cloned.1.call-done = bf16[1024,1024]{1,0:T(8,128)(2,1)} async-done(((bf16[1024,8192]{1,0:T(8,128)(2,1)}), bf16[1024,1024]{1,0:T(8,128)(2,1)}) %reduce-scatter.2.cloned.1.call-update) | async-done | bytes 2097168 | tf_op jit(solution)/shard_map/reduce_scatter | solution.py:70
  (16 shorter events, 0.2 us)
Async XLA Ops:
  6.5 234.8 %all-gather.2.cloned.1.call-start = ((), (), s32[]{:S(2)}) async-start(), calls=%async_computation.1 | async-start | bytes 17825792 | tf_op jit(solution)/shard_map/all_gather | solution.py:67
  7.3 594.1 %reduce-scatter.2.cloned.1.call-start = ((), (), s32[]{:S(2)}) async-start(), calls=%async_computation.2 | async-start | bytes 18874368 | tf_op jit(solution)/shard_map/reduce_scatter | solution.py:70
  8.1 160.0 %collective-permute-start = (bf16[6,3,1024]{2,0,1:T(8,128)(2,1)S(1)}, bf16[6,3,1024]{2,0,1:T(8,128)(2,1)S(1)}, u32[]{:S(2)}, u32[]{:S(2)}) collective-permute-start(bf16[6,3,1024]{2,0,1:T(8,128)(2,1)S(1)} %slice_bitcast_fusion), channel_id=1, source_target_pairs={{0,8},{8,16},{16,24},{24,32},{32,40},{40,48},{48,56},{56,64},{64,7... | collective-permute-start | bytes 110600 | tf_op jit(solution)/shard_map/ppermute | solution.py:12
  9.9 25.8 %slice-start = ((s8[6291456]{0:T(1024)(128)(4,1)}), s8[2097152]{0:T(1024)(128)(4,1)S(1)}, s32[]{:S(2)}) async-start(s8[6291456]{0:T(1024)(128)(4,1)} %bitcast.90), calls=%async_computation.3 | async-start | bytes 4194304
  19.5 16.2 %slice-start.1 = ((s8[6291456]{0:T(1024)(128)(4,1)}), s8[4194304]{0:T(1024)(128)(4,1)S(1)}, s32[]{:S(2)}) async-start(s8[6291456]{0:T(1024)(128)(4,1)} %bitcast.90), calls=%async_computation.4 | async-start | bytes 8388608
  31.1 204.7 %collective-permute-start.1 = (bf16[128,1024]{0,1:T(8,128)(2,1)S(1)}, bf16[128,1024]{0,1:T(8,128)(2,1)S(1)}, u32[]{:S(2)}, u32[]{:S(2)}) collective-permute-start(bf16[128,1024]{0,1:T(8,128)(2,1)S(1)} %fusion.52), channel_id=1, source_target_pairs={{0,8},{8,16},{16,24},{24,32},{32,40},{40,48},{48,56},{56,64},{64,7... | collective-permute-start | bytes 786440 | tf_op jit(solution)/shard_map/ppermute | solution.py:12
  35.8 6.1 %copy-start.3 = (f32[64,128]{1,0:T(8,128)S(1)}, f32[64,128]{1,0:T(8,128)}, u32[]{:S(2)}) copy-start(f32[64,128]{1,0:T(8,128)} %param.9) | copy-start | bytes 98308
  226.9 5.6 copy-start.1
  232.5 3.3 copy-start
  232.5 3.3 copy-start.2
  237.4 3.9 copy-start.4
Sparse Core Ops, SparseCore 0:
  9.6 124.5 all-gather.1
  273.2 328.0 reduce-scatter.1
where the time goes:
time: 610 us; the launch traced here: 608 us
  waiting for transfers between devices  329 us (54%)
  local copies, waits for them, and re-layouts  157 us (26%)
  other arithmetic  65.7 us (11%)
  matrix products  36.6 us (6%)
  between operations  13.6 us (2%)
  starting transfers between devices  6.27 us (1%)
    reduce_scatter x1, waiting for transfers between devices, on_device(): lax.psum_scatter(terms.astype(jnp.bfloat16), 'tp', scatter_dimension=1, t...  328 us
    gather x2, local copies, waits for them, and re-layouts, toeplitz(): near = jnp.where(lag >= 0, taps[:, jnp.clip(lag, 0, width - 1)], zero)  63 us
    gather x2, local copies, waits for them, and re-layouts, toeplitz(): far = jnp.where(lag < 0, taps[:, jnp.clip(lag + width, 0, width - 1)], zero)  63 us
    add x2, other arithmetic, short_conv(): total = total + weights[lag] * ext[:, span - 1 - lag:span - 1 - lag + block]  46.5 us
    dot_general x1, matrix products, on_device(): jnp.dot(mixer, lax.all_gather(out_weight, 'ctx', axis=1, tiled=True), pre...  31.7 us
  transfers between devices with their start and end apart: 4, of which 1 were waited for; matrix products, arithmetic and copies ran while one was open for 37% of the time, Pallas kernels for 0%

commit v1 on v0

v1 whole, which is shorter than its diff:
```python
import jax
import jax.numpy as jnp
from jax import lax
from jax.experimental import pallas as pl
from jax.experimental.pallas import tpu as pltpu
from jax.sharding import PartitionSpec as P

MESH = pl.DeviceIdType.MESH
F32 = jnp.float32
BF16 = jnp.bfloat16

ROWS = 1024
CH = 1024
BLK = 128
NB = ROWS // BLK
SPAN = 7
HALO = 16
GROUP = 16
LANES = 128
PER_TILE = LANES // GROUP
CHUNK = 256
NCHUNK = ROWS // CHUNK


def unit_of(kind, u):
    late, v = u // 4, u % 4
    plain = 2 * (v % 2) + v // 2
    swapped = 2 * (1 - v % 2) + v // 2
    dy0, h0 = 2 - 2 * late, plain
    dy1, h1 = 1 + 2 * (v % 2), late * plain + (1 - late) * swapped
    return dy0 + kind * (dy1 - dy0), h0 + kind * (h1 - h0)


def kernel(
    feats, starts, sw, rtaps, bias, w_ref, out_ref,
    fbuf, ext, gbuf, toep, xs, conv, mix, wts, part, got1, got2,
    f_sem, halo_ss, halo_rs, w_rs, sib_ss, zp_ss, zm_ss, x_ss, mix_ss, mix_rs,
    p_ss, got1_rs, got2_rs,
):
    c, t = lax.axis_index("ctx"), lax.axis_index("tp")
    xh, z, k = c // 8, (c // 2) % 4, c % 2
    y, xl = t // 2, t % 2
    role = (xl + z) % 2

    def dev(xh, z, k, y, xl):
        return ((xh * 4 + z) * 2 + k, y * 2 + xl)

    sib = dev(xh, z, 1 - k, y, xl)
    zp, zm = dev(xh, (z + 1) % 4, k, y, xl), dev(xh, (z + 3) % 4, k, y, xl)
    yp, ym = dev(xh, z, k, (y + 1) % 4, xl), dev(xh, z, k, (y + 3) % 4, xl)
    xp, xn, x2 = dev(xh, z, k, y, 1 - xl), dev(1 - xh, z, k, y, 1 - xl), dev(1 - xh, z, k, y, xl)
    nxt, prv = ((c + 1) % 16, t), ((c + 15) % 16, t)

    f_copies = []
    for s in range(3):
        cp = pltpu.make_async_copy(feats.at[s], fbuf.at[s, pl.ds(HALO, ROWS)], f_sem.at[s])
        cp.start()
        f_copies.append(cp)

    barrier = pltpu.get_barrier_semaphore()
    for d in (sib, zp, zm, yp, ym, xp, xn, x2, prv):
        pl.semaphore_signal(barrier, inc=1, device_id=d, device_id_type=MESH)
    pl.semaphore_wait(barrier, 9)

    def remote(src, dst, ss, rs, d):
        return pltpu.make_async_remote_copy(
            src_ref=src, dst_ref=dst, send_sem=ss, recv_sem=rs, device_id=d, device_id_type=MESH
        )

    dy_own = (2 * xh + z // 2 - y + 4) % 4

    def w_piece(h):
        return w_ref.at[:, pl.ds(h * LANES, LANES)]

    def slot(dy, h, r, core):
        return wts.at[dy, h, r, :, pl.ds(pl.multiple_of(core * LANES, LANES), LANES)]

    def x_copy(h, r, d, i):
        return remote(w_piece(h), slot(dy_own, h, r, k), x_ss.at[h, i], w_rs.at[dy_own, h, r, k], d)

    halo_f = remote(
        feats.at[:, pl.ds(ROWS - HALO, HALO)], fbuf.at[:, pl.ds(0, HALO)], halo_ss.at[0], halo_rs.at[0], nxt
    )
    halo_f.start()

    @pl.when(role == 0)
    def _():
        for h in (0, 2, 1, 3):
            pltpu.make_async_copy(w_piece(h), slot(dy_own, h, 0, k), w_rs.at[dy_own, h, 0, k]).start()
            x_copy(h, 0, x2, 0).start()

    @pl.when(role == 1)
    def _():
        for h in (0, 2, 1, 3):
            x_copy(h, 1, xp, 0).start()
            x_copy(h, 1, xn, 1).start()

    def sib_copy(dy, h, r):
        here = slot(dy, h, r, k)
        return remote(here, here, sib_ss.at[dy, h, r], w_rs.at[dy, h, r, k], sib)

    def zp_copy(dy, h, r):
        here = slot(dy, h, r, k)
        return remote(here, here, zp_ss.at[dy, h, r], w_rs.at[dy, h, r, k], zp)

    def zm_copy(dy, h, r):
        here = slot(dy, h, r, k)
        return remote(here, here, zm_ss.at[dy, h, r], w_rs.at[dy, h, r, k], zm)

    def w_wait(dy, h, r, core):
        here = slot(dy, h, r, core)
        remote(here, here, sib_ss.at[dy, h, r], w_rs.at[dy, h, r, core], sib).wait_recv()

    kind_here = (z // 2 + y) % 2
    kind_below = (((z + 3) % 4) // 2 + y) % 2

    def spread(lo, hi):
        @pl.when(role == 0)
        def _():
            def body(u, _):
                dy, h = unit_of(kind_here, u)
                for r in range(2):
                    w_wait(dy, h, r, k)
                    zp_copy(dy, h, r).start()
                    zm_copy(dy, h, r).start()
                    sib_copy(dy, h, r).start()
                return 0

            lax.fori_loop(lo, hi, body, 0)

    def relay(lo, hi):
        @pl.when(role == 0)
        def _():
            def body(u, _):
                dy, h = unit_of(1 - kind_here, u)
                for r in range(2):
                    w_wait(dy, h, r, k)
                    sib_copy(dy, h, r).start()
                return 0

            lax.fori_loop(lo, hi, body, 0)

        @pl.when(role == 1)
        def _():
            def body(u, _):
                dya, ha = unit_of(kind_below, u)
                dyb, hb = unit_of(1 - kind_below, u)
                for r in range(2):
                    w_wait(dya, ha, r, k)
                    if r == 0:
                        zp_copy(dya, ha, r).start()
                    sib_copy(dya, ha, r).start()
                    w_wait(dyb, hb, r, k)
                    if r == 1:
                        zm_copy(dyb, hb, r).start()
                    sib_copy(dyb, hb, r).start()
                return 0

            lax.fori_loop(lo, hi, body, 0)

    def toep_body(g, _):
        row = jnp.broadcast_to(rtaps[pl.ds(g, 1)], (BLK, 2 * BLK))
        toep[g] = pltpu.roll(row, 1, 1, stride=1, stride_axis=0).astype(BF16)
        return 0

    lax.fori_loop(0, CH // GROUP, toep_body, 0)

    first = (c > 0).astype(F32)

    def keep_of(b):
        kept = (1 - starts[b]).astype(F32)
        return kept * jnp.where(b == 0, first, 1.0)

    def short(s, b, keep, lanes):
        tail = fbuf[s, pl.ds(pl.multiple_of(b * BLK, BLK), HALO), lanes].astype(F32)
        ext[s, pl.ds(0, 8), lanes] = tail[8:] * keep
        ext[s, pl.ds(8, BLK), lanes] = fbuf[
            s, pl.ds(pl.multiple_of(b * BLK + HALO, HALO), BLK), lanes
        ].astype(F32)
        total = sw[s, pl.ds(0, 1), lanes] * ext[s, pl.ds(8, BLK), lanes]
        for j in range(1, SPAN):
            total += sw[s, pl.ds(j, 1), lanes] * ext[s, pl.ds(8 - j, BLK), lanes]
        return total

    def lanes_of(lt):
        return pl.ds(pl.multiple_of(lt * LANES, LANES), LANES)

    def gate(b):
        keep = keep_of(b)

        def body(lt, _):
            lanes = lanes_of(lt)
            gbuf[b + 1, :, lanes] = (short(1, b, keep, lanes) * short(2, b, keep, lanes)).astype(BF16)
            return 0

        lax.fori_loop(0, CH // LANES, body, 0)

    for cp in f_copies:
        cp.wait()
    gate(NB - 1)
    halo_g = remote(gbuf.at[NB], gbuf.at[0], halo_ss.at[1], halo_rs.at[1], nxt)
    halo_g.start()

    def gate_body(i, _):
        gate(NB - 2 - i)
        return 0

    lax.fori_loop(0, NB - 2, gate_body, 0)
    halo_f.wait_recv()
    gate(0)
    spread(0, 4)

    def mix_copy(m):
        rows = pl.ds(m * CHUNK, CHUNK)
        return remote(mix.at[0, rows], mix.at[1, rows], mix_ss.at[m], mix_rs.at[m], xp)

    lane_group = lax.broadcasted_iota(jnp.int32, (BLK, 2 * LANES), 1) % LANES // GROUP

    def mix_pair(b0):
        keeps = [keep_of(b0), keep_of(b0 + 1)]

        def body(lt, _):
            lanes = lanes_of(lt)
            for i in range(2):
                cols = pl.ds(i * LANES, LANES)
                xs[pl.ds(0, BLK), cols] = (gbuf[b0 + i, :, lanes].astype(F32) * keeps[i]).astype(BF16)
                xs[pl.ds(BLK, BLK), cols] = gbuf[b0 + i + 1, :, lanes]
            mats = toep[pl.ds(lt * PER_TILE, PER_TILE)].reshape(PER_TILE * BLK, 2 * BLK)
            every = jnp.dot(mats, xs[...], preferred_element_type=F32)
            every = every.reshape(PER_TILE, BLK, 2 * LANES)
            picked = every[0]
            for g in range(1, PER_TILE):
                picked = jnp.where(lane_group == g, every[g], picked)
            conv[...] = picked
            for i in range(2):
                gated = gbuf[b0 + i + 1, :, lanes].astype(F32)
                query = short(0, b0 + i, keeps[i], lanes)
                direct = conv[:, pl.ds(i * LANES, LANES)] + bias[:, lanes] * gated
                mix[0, pl.ds(pl.multiple_of((b0 + i) * BLK, BLK), BLK), lanes] = (query * direct).astype(BF16)
            return 0

        lax.fori_loop(0, CH // LANES, body, 0)

    chunk_at = [NCHUNK - 1 - i for i in range(NCHUNK)]

    def chunk_body(i, _):
        m = NCHUNK - 1 - i
        mix_pair(2 * m)
        mix_copy(m).start()
        return 0

    lax.fori_loop(0, NCHUNK - 1, chunk_body, 0)
    spread(4, 8)
    halo_g.wait_recv()
    chunk_body(NCHUNK - 1, 0)

    def rows_of(m):
        return pl.ds(pl.multiple_of(m * CHUNK, CHUNK), CHUNK)

    def project(dy, h, m):
        rows = rows_of(m)
        total = jnp.dot(mix[0, rows], wts[dy, h, 0], preferred_element_type=F32)
        return total + jnp.dot(mix[1, rows], wts[dy, h, 1], preferred_element_type=F32)

    def to_y(dy):
        return dev(xh, z, k, (y + dy) % 4, xl)

    def far_copy(v, m):
        dy, h = unit_of(0, v)
        here = part.at[dy, h, rows_of(m)]
        return remote(here, got1.at[h, rows_of(m)], p_ss.at[dy, h, m], got1_rs.at[h, m], to_y(1 + 2 * (v % 2)))

    def near_copy(u, m):
        dy, h = unit_of(1, u)
        here = part.at[dy, h, rows_of(m)]
        there = got2.at[dy // 2, h, rows_of(m)]
        return remote(here, there, p_ss.at[dy, h, m], got2_rs.at[dy // 2, h, m], to_y(dy))

    def got1_wait(h, m):
        there = got1.at[h, rows_of(m)]
        remote(there, there, p_ss.at[0, h, m], got1_rs.at[h, m], yp).wait_recv()

    def got2_wait(side, h, m):
        there = got2.at[side, h, rows_of(m)]
        remote(there, there, p_ss.at[0, h, m], got2_rs.at[side, h, m], yp).wait_recv()

    def sib_wait(u):
        for kind in range(2):
            dy, h = unit_of(kind, u)
            for r in range(2):
                w_wait(dy, h, r, 1 - k)

    for s in range(4):
        relay(s, s + 1)
        sib_wait(s)
        mix_copy(chunk_at[s]).wait_recv()

        def early_body(n, _):
            u = jnp.minimum(n, s)
            m = NCHUNK - 1 - jnp.where(n <= s, s, n - s - 1)
            dy, h = unit_of(0, u)
            part[dy, h, rows_of(m)] = project(dy, h, m).astype(BF16)
            far_copy(u, m).start()
            dy, h = unit_of(1, u)
            part[dy, h, rows_of(m)] = project(dy, h, m).astype(BF16)
            near_copy(u, m).start()
            return 0

        lax.fori_loop(0, 2 * s + 1, early_body, 0)

    def late_step(u, _):
        relay(u, u + 1)
        sib_wait(u)

        def late_body(i, _):
            m = NCHUNK - 1 - i
            dy, h = unit_of(1, u)
            got1_wait(h, m)
            total = project(dy, h, m) + got1[h, rows_of(m)].astype(F32)
            part[dy, h, rows_of(m)] = total.astype(BF16)
            near_copy(u, m).start()
            dy, h = unit_of(0, u)
            part[dy, h, rows_of(m)] = project(dy, h, m).astype(BF16)
            return 0

        lax.fori_loop(0, NCHUNK, late_body, 0)
        return 0

    lax.fori_loop(4, 8, late_step, 0)

    for h in (0, 2, 1, 3):
        def sum_body(i, _):
            m = NCHUNK - 1 - i
            rows = rows_of(m)
            got2_wait(0, h, m)
            got2_wait(1, h, m)
            total = part[0, h, rows].astype(F32) + got2[0, h, rows].astype(F32) + got2[1, h, rows].astype(F32)
            total = total.astype(BF16)
            for core in range(2):
                out_ref[rows, pl.ds(core * 512 + h * LANES, LANES)] = total[:, core * LANES : (core + 1) * LANES]
            return 0

        lax.fori_loop(0, NCHUNK, sum_body, 0)

    halo_f.wait_send()
    halo_g.wait_send()
    for m in range(NCHUNK):
        mix_copy(m).wait_send()

    def sent_body(u, _):
        for kind in range(2):
            dy, h = unit_of(kind, u)
            for r in range(2):
                sib_copy(dy, h, r).wait_send()

        @pl.when(role == 0)
        def _():
            dy, h = unit_of(kind_here, u)
            for r in range(2):
                zp_copy(dy, h, r).wait_send()
                zm_copy(dy, h, r).wait_send()

        @pl.when(role == 1)
        def _():
            dya, ha = unit_of(kind_below, u)
            dyb, hb = unit_of(1 - kind_below, u)
            zp_copy(dya, ha, 0).wait_send()
            zm_copy(dyb, hb, 1).wait_send()

        for m in range(NCHUNK):
            near_copy(u, m).wait_send()
        return 0

    lax.fori_loop(0, 8, sent_body, 0)

    def far_sent_body(v, _):
        for m in range(NCHUNK):
            far_copy(v, m).wait_send()

        @pl.when(role == 0)
        def _():
            x_copy(v, 0, x2, 0).wait_send()

        @pl.when(role == 1)
        def _():
            x_copy(v, 1, xp, 0).wait_send()
            x_copy(v, 1, xn, 1).wait_send()

        return 0

    lax.fori_loop(0, 4, far_sent_body, 0)


def on_device(features, contig_starts, short_filter, medium_filter, filter_bias, out_weight):
    vmem = pl.BlockSpec(memory_space=pltpu.VMEM)
    hbm = pl.BlockSpec(memory_space=pl.ANY)
    dma = pltpu.SemaphoreType.DMA
    taps = medium_filter.astype(BF16).astype(F32)[:, ::-1]
    taps = jnp.concatenate([taps, jnp.zeros_like(taps)], axis=1)
    return pl.pallas_call(
        kernel,
        out_shape=jax.ShapeDtypeStruct((ROWS, CH), BF16),
        in_specs=[hbm, pl.BlockSpec(memory_space=pltpu.SMEM), vmem, vmem, vmem, hbm],
        out_specs=vmem,
        scratch_shapes=[
            pltpu.VMEM((3, HALO + ROWS, CH), BF16),
            pltpu.VMEM((3, 8 + BLK, CH), F32),
            pltpu.VMEM((NB + 1, BLK, CH), BF16),
            pltpu.VMEM((CH // GROUP, BLK, 2 * BLK), BF16),
            pltpu.VMEM((2 * BLK, 2 * LANES), BF16),
            pltpu.VMEM((BLK, 2 * LANES), F32),
            pltpu.VMEM((2, ROWS, CH), BF16),
            pltpu.VMEM((4, 4, 2, CH, 2 * LANES), BF16),
            pltpu.VMEM((4, 4, ROWS, 2 * LANES), BF16),
            pltpu.VMEM((4, ROWS, 2 * LANES), BF16),
            pltpu.VMEM((2, 4, ROWS, 2 * LANES), BF16),
            dma((3,)),
            dma((2,)),
            dma((2,)),
            dma((4, 4, 2, 2)),
            dma((4, 4, 2)),
            dma((4, 4, 2)),
            dma((4, 4, 2)),
            dma((4, 2)),
            dma((NCHUNK,)),
            dma((NCHUNK,)),
            dma((4, 4, NCHUNK)),
            dma((4, NCHUNK)),
            dma((2, 4, NCHUNK)),
        ],
        compiler_params=pltpu.CompilerParams(
            collective_id=0, has_side_effects=True, vmem_limit_bytes=60 * 1024 * 1024
        ),
        cost_estimate=pl.CostEstimate(
            flops=2 * ROWS * 2048 * 4096, bytes_accessed=16 * 1024 * 1024, transcendentals=0
        ),
    )(
        jnp.transpose(features, (1, 0, 2)),
        contig_starts,
        jnp.transpose(short_filter, (1, 0, 2)),
        taps,
        filter_bias.reshape(1, CH),
        out_weight,
    )


def solution(mesh):
    in_specs = (
        P("ctx", None, "tp"),
        P("ctx"),
        P(None, None, "tp"),
        P("tp", None),
        P("tp"),
        P("tp", "ctx"),
    )
    out_specs = P("ctx", "tp")
    return jax.shard_map(
        on_device, mesh=mesh, in_specs=in_specs, out_specs=out_specs, check_vma=False
    )
```

time: 610 us -> 175 us (0.29)
  the two profiles are of different devices: /device:TPU:16 before, /device:TPU:1 now
where the time goes in v1:
time: 175 us
  Pallas kernels  170 us (97%)
  local copies, waits for them, and re-layouts  3.8 us (2%)
    pallas_call x1, Pallas kernels, on_device(): pl.pallas_call(kernel, out_shape=jax.ShapeDtypeStruct((ROWS, CH), BF16),...  170 us

profile of v1, /device:TPU:1, one launch (start us, length us, event | category | flops | bytes accessed | tf_op | source)
XLA Modules:
  0.0 174.9 jit_solution(8717445241386262615)
XLA Ops:
  0.0 0.8 convert_convert_fusion
  0.8 0.1 rev.3
  0.8 0.6 concatenate.3.rtaps
  1.5 170.3 %shard_map.64 = bf16[1024,1024]{1,0:T(8,128)(2,1)} custom-call(bf16[3,1024,1024]{2,1,0:T(8,128)(2,1)} %bitcast.3, s32[8]{0:T(128)} %starts.1, f32[3,7,1024]{2,1,0:T(8,128)} %bitcast.4, f32[64,256]{1,0:T(8,128)} %concatenate.3.rtaps, f32[1,1024]{1,0:T(1,128)} %bitcast.5, bf16[1024,512]{1,0:T(8,128)(2,1)} %w_ref.1), custom_call_target="tpu_custom_call" | custom-call | flops 17179869184 | bytes 16777216 | tf_op jit(solution)/shard_map/pallas_call | solution.py:400
  171.8 3.1 %copy.8 = bf16[1024,1024]{1,0:T(8,128)(2,1)} copy(bf16[1024,1024]{1,0:T(8,128)(2,1)} %shard_map.64) | data formatting | bytes 4194304

commit v2 on v1

--- a/solution.py
+++ b/solution.py
@@ -22,19 +22,264 @@
 NCHUNK = ROWS // CHUNK
 
 
-def unit_of(kind, u):
-    late, v = u // 4, u % 4
-    plain = 2 * (v % 2) + v // 2
-    swapped = 2 * (1 - v % 2) + v // 2
-    dy0, h0 = 2 - 2 * late, plain
-    dy1, h1 = 1 + 2 * (v % 2), late * plain + (1 - late) * swapped
-    return dy0 + kind * (dy1 - dy0), h0 + kind * (h1 - h0)
+TRANSFERS = (
+    ((2, 0, 0, 0), (2, 0, 0, 0), (2, 0, 0, 0), (2, 0, 0, 0), (2, 1, 0, 0), (2, 1, 0, 0), (2, 1, 0, 0), (2, 1, 0, 0)),
+    ((2, 0, 1, 0), (2, 0, 1, 0), (2, 0, 1, 0), (2, 0, 1, 0), (2, 1, 0, 0), (2, 1, 0, 0), (2, 1, 0, 0), (2, 1, 0, 0)),
+    ((2, 0, 1, 0), (2, 0, 1, 0), (2, 0, 1, 0), (2, 0, 1, 0), (2, 1, 0, 0), (2, 1, 0, 0), (2, 1, 0, 0), (2, 1, 0, 0)),
+    ((2, 0, 1, 0), (2, 0, 1, 0), (2, 0, 1, 0), (2, 0, 1, 0), (2, 1, 0, 0), (2, 1, 0, 0), (2, 1, 0, 0), (2, 1, 0, 0)),
+    ((2, 1, 3, 0), (2, 1, 3, 0), (2, 1, 3, 0), (2, 1, 3, 0), (2, 3, 0, 0), (2, 3, 0, 0), (2, 3, 0, 0), (2, 3, 0, 0)),
+    ((2, 1, 3, 0), (2, 1, 3, 0), (2, 1, 3, 0), (2, 1, 3, 0), (2, 3, 1, 1), (2, 3, 0, 1), (2, 3, 1, 1), (2, 3, 1, 0)),
+    ((3, 1, 3, 0), (3, 1, 3, 0), (3, 1, 3, 0), (3, 1, 3, 0), (3, 3, 1, 1), (3, 3, 0, 1), (3, 3, 1, 1), (3, 3, 1, 0)),
+    ((3, 2, 5, 0), (3, 2, 5, 0), (3, 2, 6, 0), (3, 2, 6, 0), (3, 5, 1, 1), (3, 5, 0, 1), (3, 5, 1, 1), (3, 5, 1, 0)),
+    ((4, 2, 5, 0), (4, 2, 5, 0), (4, 2, 6, 0), (4, 2, 6, 0), (4, 5, 2, 2), (4, 5, 1, 2), (4, 5, 3, 2), (4, 5, 3, 0)),
+    ((4, 3, 5, 0), (4, 3, 5, 0), (4, 3, 6, 0), (4, 3, 6, 0), (4, 5, 2, 2), (4, 5, 1, 2), (4, 5, 3, 2), (4, 5, 3, 0)),
+    ((4, 3, 5, 0), (4, 3, 6, 0), (4, 3, 7, 0), (4, 3, 7, 0), (4, 5, 3, 4), (4, 5, 2, 4), (4, 5, 4, 3), (4, 5, 4, 2)),
+    ((4, 3, 5, 0), (4, 3, 6, 0), (4, 3, 7, 0), (4, 3, 7, 0), (4, 5, 3, 4), (4, 5, 2, 4), (4, 5, 4, 3), (4, 5, 4, 2)),
+    ((4, 4, 5, 0), (4, 4, 6, 0), (4, 4, 7, 0), (4, 4, 7, 0), (4, 5, 3, 4), (4, 5, 2, 4), (4, 5, 4, 3), (4, 5, 4, 2)),
+    ((4, 4, 6, 2), (4, 4, 8, 0), (4, 4, 9, 0), (4, 4, 9, 0), (4, 5, 4, 5), (4, 5, 4, 4), (4, 5, 5, 4), (4, 5, 6, 2)),
+    ((4, 4, 7, 4), (4, 4, 8, 4), (4, 4, 10, 2), (4, 4, 10, 2), (4, 7, 6, 6), (4, 7, 4, 8), (4, 7, 6, 6), (4, 7, 8, 4)),
+    ((4, 4, 7, 6), (4, 4, 11, 4), (4, 4, 12, 4), (4, 4, 12, 4), (4, 7, 6, 8), (4, 7, 5, 8), (4, 7, 8, 6), (4, 7, 8, 4)),
+    ((4, 4, 14, 6), (4, 4, 12, 6), (4, 4, 13, 4), (4, 4, 13, 4), (4, 7, 7, 9), (4, 7, 6, 9), (4, 7, 9, 7), (4, 7, 9, 6)),
+    ((4, 4, 15, 8), (4, 4, 12, 6), (4, 4, 13, 6), (4, 4, 13, 4), (4, 8, 7, 10), (4, 8, 6, 10), (4, 8, 10, 7), (4, 8, 10, 6)),
+    ((4, 4, 15, 8), (4, 4, 12, 8), (4, 4, 15, 6), (4, 4, 15, 6), (4, 8, 8, 11), (4, 8, 7, 12), (4, 8, 11, 8), (4, 8, 12, 6)),
+    ((4, 4, 15, 9), (4, 4, 13, 8), (4, 4, 15, 6), (4, 4, 16, 6), (4, 8, 9, 12), (4, 8, 7, 12), (4, 8, 12, 9), (4, 8, 12, 7)),
+    ((4, 4, 16, 9), (4, 4, 16, 10), (4, 4, 16, 7), (4, 4, 16, 6), (4, 8, 11, 12), (4, 8, 13, 13), (4, 8, 12, 11), (4, 8, 13, 13)),
+    ((4, 4, 16, 10), (4, 4, 16, 10), (4, 4, 16, 7), (4, 4, 16, 7), (4, 8, 11, 13), (4, 8, 13, 13), (4, 8, 13, 11), (4, 8, 13, 13)),
+    ((4, 4, 16, 10), (4, 4, 16, 10), (4, 4, 16, 8), (4, 4, 16, 8), (4, 8, 11, 13), (4, 8, 13, 13), (4, 8, 13, 11), (4, 8, 13, 13)),
+    ((4, 4, 16, 10), (4, 4, 16, 10), (4, 4, 16, 10), (4, 4, 16, 8), (4, 8, 13, 13), (4, 8, 13, 13), (4, 8, 13, 13), (4, 8, 15, 14)),
+    ((4, 4, 16, 10), (4, 4, 16, 12), (4, 4, 16, 10), (4, 4, 16, 10), (4, 8, 13, 15), (4, 8, 14, 15), (4, 8, 15, 13), (4, 8, 15, 14)),
+    ((4, 4, 16, 12), (4, 4, 16, 12), (4, 4, 16, 12), (4, 4, 16, 10), (4, 8, 15, 16), (4, 8, 15, 16), (4, 8, 16, 15), (4, 8, 15, 14)),
+    ((4, 4, 16, 12), (4, 4, 16, 12), (4, 4, 16, 12), (4, 4, 16, 12), (4, 8, 15, 16), (4, 8, 15, 16), (4, 8, 16, 15), (4, 8, 16, 15)),
+    ((4, 4, 16, 12), (4, 4, 16, 13), (4, 4, 16, 14), (4, 4, 16, 12), (4, 8, 15, 16), (4, 8, 15, 16), (4, 8, 16, 15), (4, 8, 16, 15)),
+    ((4, 4, 16, 13), (4, 4, 16, 13), (4, 4, 16, 16), (4, 4, 16, 14), (4, 8, 16, 16), (4, 8, 16, 16), (4, 8, 16, 16), (4, 8, 16, 16)),
+    ((4, 4, 16, 14), (4, 4, 16, 14), (4, 4, 16, 16), (4, 4, 16, 16), (4, 8, 16, 16), (4, 8, 16, 16), (4, 8, 16, 16), (4, 8, 16, 16)),
+    ((4, 4, 16, 14), (4, 4, 16, 14), (4, 4, 16, 16), (4, 4, 16, 16), (4, 8, 16, 16), (4, 8, 16, 16), (4, 8, 16, 16), (4, 8, 16, 16)),
+    ((4, 4, 16, 16), (4, 4, 16, 16), (4, 4, 16, 16), (4, 4, 16, 16), (4, 8, 16, 16), (4, 8, 16, 16), (4, 8, 16, 16), (4, 8, 16, 16)),
+    ((4, 4, 16, 16), (4, 4, 16, 16), (4, 4, 16, 16), (4, 4, 16, 16), (4, 8, 16, 16), (4, 8, 16, 16), (4, 8, 16, 16), (4, 8, 16, 16)),
+)
+PHASES = (
+    (
+        ((0, 1), 1, (3, 7)),
+        ((0, 4), 1, (3, 19)),
+        ((8, 9), 1, (35, 39)),
+        ((8, 9), 1, (35, 39)),
+        ((0, 8), 1, (3, 35)),
+        ((0, 8), 1, (3, 35)),
+        ((0, 8), 1, (3, 35)),
+        ((0, 8), 1, (3, 35)),
+    ),
+    (
+        ((2, 8), 0, (11, 35)),
+        ((1, 5), 0, (7, 23)),
+        ((10, 11), 0, (43, 47)),
+        ((10, 11), 0, (43, 47)),
+        ((9, 1), 0, (39, 7)),
+        ((9, 1), 0, (39, 7)),
+        ((9, 1), 0, (39, 7)),
+        ((9, 10), 0, (39, 43)),
+    ),
+    (
+        ((9,), 1, (39, 2, 6, 10, 34)),
+        ((8, 9), 0, (35, 39)),
+        ((12, 0), 0, (51, 3)),
+        ((12, 0), 0, (51, 3)),
+        ((10, 2), 0, (43, 11)),
+        ((10, 11), 0, (43, 47)),
+        ((10, 2), 0, (43, 11)),
+        ((1, 11), 0, (7, 47)),
+    ),
+    (
+        ((10,), 0, (38, 43, 42)),
+        ((2,), 1, (11, 2, 18, 6, 22)),
+        ((1, 13), 0, (7, 55)),
+        ((13, 1), 0, (55, 7)),
+        ((11,), 1, (47, 2, 34, 38, 6)),
+        ((), 1, (2, 34, 38, 6, 42)),
+        ((11,), 1, (47, 2, 34, 38, 6)),
+        ((), 1, (2, 34, 38, 42, 6)),
+    ),
+    (
+        ((3,), 0, (15, 14)),
+        ((), 0, (34, 38, 10)),
+        ((), 1, (34, 38, 42, 46, 2)),
+        ((), 1, (34, 38, 42, 46, 2)),
+        ((), 0, (42, 10, 46)),
+        ((2,), 0, (46, 11, 10)),
+        ((), 0, (42, 10, 46)),
+        ((2,), 0, (46, 11, 10)),
+    ),
+    (
+        ((4,), 0, (19, 18)),
+        ((10,), 0, (43, 42)),
+        ((), 0, (6, 50)),
+        ((), 0, (6, 50, 54)),
+        ((12,), 0, (51, 50)),
+        ((12,), 0, (51, 50)),
+        ((12,), 0, (51, 50)),
+        ((12,), 0, (51, 50)),
+    ),
+    (
+        ((5,), 0, (23, 22)),
+        ((11,), 0, (47, 46)),
+        ((2,), 0, (11, 10, 54)),
+        ((2,), 0, (11, 10)),
+        ((3,), 0, (15, 14)),
+        ((13,), 0, (55, 54)),
+        ((3,), 0, (15, 14)),
+        ((13,), 0, (55, 54)),
+    ),
+    (
+        ((6,), 0, (27, 26)),
+        ((3,), 0, (15, 14)),
+        ((14,), 0, (59, 58)),
+        ((14,), 0, (59, 58)),
+        ((13,), 0, (55, 54)),
+        ((), 1, (1, 33, 37, 5, 41)),
+        ((13,), 0, (55, 54)),
+        ((), 1, (1, 33, 37, 41, 5)),
+    ),
+    (
+        ((11,), 0, (47, 46)),
+        ((6,), 0, (27, 26)),
+        ((15,), 1, (63, 33, 37, 41, 45)),
+        ((15,), 1, (63, 33, 37, 41, 45)),
+        ((), 1, (1, 33, 37, 5, 41)),
+        ((), 0, (45, 9)),
+        ((), 1, (1, 33, 37, 5, 41)),
+        ((), 0, (45, 9)),
+    ),
+    (
+        ((7,), 0, (31, 30)),
+        ((7,), 0, (31, 30)),
+        ((), 0, (1, 5, 9, 62)),
+        ((), 0, (1, 5, 9, 62, 49)),
+        ((), 0, (9, 45, 13)),
+        ((3,), 0, (15, 14, 13)),
+        ((), 0, (9, 45, 13)),
+        ((3,), 0, (15, 14, 13)),
+    ),
+    (
+        ((12,), 0, (51, 50)),
+        ((12,), 0, (51, 50)),
+        ((3,), 0, (15, 14, 13, 53, 49)),
+        ((3,), 0, (15, 14, 13)),
+        ((4,), 0, (19, 18, 17)),
+        ((4,), 0, (19, 18, 17)),
+        ((4,), 0, (19, 18, 17)),
+        ((4,), 0, (19, 18, 17)),
+    ),
+    (
+        ((), 1, (1, 5, 9, 33, 37)),
+        ((), 1, (1, 17, 5, 21, 33)),
+        ((4,), 0, (57, 19, 18, 17)),
+        ((), 1, (32, 36, 40, 44, 0)),
+        ((5,), 0, (23, 22, 21)),
+        ((5,), 0, (23, 22, 21, 49, 53)),
+        ((5,), 0, (23, 22, 21)),
+        ((5,), 0, (23, 22, 21, 53, 49)),
+    ),
+    (
+        ((), 0, (41, 13, 17, 21, 25)),
+        ((), 0, (37, 9, 41, 45, 13)),
+        ((), 1, (32, 36, 40, 44, 0)),
+        ((), 0, (4, 8, 12, 53, 57)),
+        ((14,), 0, (59, 58, 53)),
+        ((6,), 0, (27, 26, 25)),
+        ((14,), 0, (59, 58, 53)),
+        ((14,), 0, (59, 58)),
+    ),
+    (
+        ((), 0, (45, 29)),
+        ((), 0, (25, 29)),
+        ((), 0, (4, 8, 12, 16, 61)),
+        ((4,), 0, (19, 18, 17, 16, 61)),
+        ((), 1, (0, 32, 36, 4, 40)),
+        ((14,), 0, (59, 58)),
+        ((), 1, (0, 32, 36, 4, 40)),
+        ((6,), 0, (27, 26, 25)),
+    ),
+    (
+        ((13,), 0, (55, 54)),
+        ((13,), 0, (55, 54)),
+        ((5,), 0, (23, 22, 21, 20)),
+        ((5,), 0, (48, 23, 22, 21, 20)),
+        ((), 0, (8, 44, 12, 16, 20)),
+        ((), 1, (0, 32, 36, 4, 40)),
+        ((), 0, (8, 44, 12, 16, 20)),
+        ((), 1, (0, 32, 36, 40, 4)),
+    ),
+    (
+        ((), 1, (0, 4, 8, 32, 36)),
+        ((), 1, (0, 16, 4, 20, 32)),
+        ((6,), 0, (27, 26, 25, 24, 52)),
+        ((), 0, (52, 56)),
+        ((6,), 0, (49, 27, 26, 25, 24)),
+        ((), 0, (44, 8, 12, 16, 20)),
+        ((6,), 0, (49, 27, 26, 25, 24)),
+        ((), 0, (44, 8, 12, 16, 20)),
+    ),
+    (
+        ((), 0, (40, 12, 16, 20, 24)),
+        ((), 0, (36, 8, 40, 44, 12)),
+        ((7,), 0, (48, 31, 30, 29, 28)),
+        ((6,), 0, (27, 26, 25, 24, 60)),
+        ((15,), 0, (63, 62, 57, 61)),
+        ((), 0, (24, 57)),
+        ((15,), 0, (63, 62, 57, 61)),
+        ((), 0, (24, 57)),
+    ),
+    (
+        ((), 0, (44, 28, 53, 49)),
+        ((), 0, (24, 28, 49, 53)),
+        ((), 0, (56, 60)),
+        ((7,), 0, (31, 30, 29, 28)),
+        ((7,), 0, (31, 30, 29, 28, 48)),
+        ((15,), 0, (63, 62, 61)),
+        ((7,), 0, (31, 30, 29, 28, 48)),
+        ((15,), 0, (63, 62, 61)),
+    ),
+    (
+        ((14,), 0, (59, 58, 57)),
+        ((14,), 0, (59, 58, 57)),
+        ((), 0, ()),
+        ((), 0, ()),
+        ((), 0, (52, 56, 60)),
+        ((7,), 0, (31, 30, 29, 28, 48)),
+        ((), 0, (52, 56, 60)),
+        ((7,), 0, (31, 30, 29, 28, 48)),
+    ),
+    (
+        ((15,), 0, (63, 62, 61, 52, 60)),
+        ((15,), 0, (63, 62, 61, 48, 52)),
+        ((), 0, ()),
+        ((), 0, ()),
+        ((), 0, ()),
+        ((), 0, (52, 56, 60)),
+        ((), 0, ()),
+        ((), 0, (52, 56, 60)),
+    ),
+    (
+        ((), 0, (48, 56)),
+        ((), 0, (56, 60)),
+        ((), 0, ()),
+        ((), 0, ()),
+        ((), 0, ()),
+        ((), 0, ()),
+        ((), 0, ()),
+        ((), 0, ()),
+    ),
+)
+
+
+def quarter(dy, i):
+    odd = dy % 2
+    return (1 - odd) * (2 * (i % 2) + i // 2) + odd * ((i + 3 - dy) % 4)
 
 
 def kernel(
     feats, starts, sw, rtaps, bias, w_ref, out_ref,
-    fbuf, ext, gbuf, toep, xs, conv, mix, wts, part, got1, got2,
-    f_sem, halo_ss, halo_rs, w_rs, sib_ss, zp_ss, zm_ss, x_ss, mix_ss, mix_rs,
+    passing, fbuf, ext, gbuf, toep, xs, conv, mix, wts, part, got1, got2,
+    f_sem, halo_ss, halo_rs, pass_rs, pass_ss, zx_ss, w_rs, sib_ss, zp_ss, zm_ss, x_ss, mix_ss, mix_rs,
     p_ss, got1_rs, got2_rs,
 ):
     c, t = lax.axis_index("ctx"), lax.axis_index("tp")
@@ -48,7 +293,7 @@
     sib = dev(xh, z, 1 - k, y, xl)
     zp, zm = dev(xh, (z + 1) % 4, k, y, xl), dev(xh, (z + 3) % 4, k, y, xl)
     yp, ym = dev(xh, z, k, (y + 1) % 4, xl), dev(xh, z, k, (y + 3) % 4, xl)
-    xp, xn, x2 = dev(xh, z, k, y, 1 - xl), dev(1 - xh, z, k, y, 1 - xl), dev(1 - xh, z, k, y, xl)
+    xp, xn = dev(xh, z, k, y, 1 - xl), dev(1 - xh, z, k, y, 1 - xl)
     nxt, prv = ((c + 1) % 16, t), ((c + 15) % 16, t)
 
     f_copies = []
@@ -58,9 +303,9 @@
         f_copies.append(cp)
 
     barrier = pltpu.get_barrier_semaphore()
-    for d in (sib, zp, zm, yp, ym, xp, xn, x2, prv):
+    for d in (sib, zp, zm, yp, ym, xp, xn, prv):
         pl.semaphore_signal(barrier, inc=1, device_id=d, device_id_type=MESH)
-    pl.semaphore_wait(barrier, 9)
+    pl.semaphore_wait(barrier, 8)
 
     def remote(src, dst, ss, rs, d):
         return pltpu.make_async_remote_copy(
@@ -75,8 +320,32 @@
     def slot(dy, h, r, core):
         return wts.at[dy, h, r, :, pl.ds(pl.multiple_of(core * LANES, LANES), LANES)]
 
-    def x_copy(h, r, d, i):
-        return remote(w_piece(h), slot(dy_own, h, r, k), x_ss.at[h, i], w_rs.at[dy_own, h, r, k], d)
+    def x_copy(i, side):
+        h = quarter(dy_own, i)
+        return remote(
+            w_piece(h), slot(dy_own, h, 1, k), x_ss.at[i, side], w_rs.at[dy_own, h, 1, k], (xp, xn)[side]
+        )
+
+    def pass_copy(i):
+        h = quarter(dy_own, i)
+        return remote(w_piece(h), passing.at[i], x_ss.at[i, 0], pass_rs.at[i], xp)
+
+    def z_pass_copy(i, side):
+        h = quarter(dy_own, i)
+        return remote(
+            w_piece(h), passing.at[4 * side + i], zx_ss.at[i, side], pass_rs.at[4 * side + i], (zp, zm)[side]
+        )
+
+    def z_onward_copy(i, side):
+        dy = (2 * xh + ((z + 3 + 2 * side) % 4) // 2 - y + 4) % 4
+        h = quarter(dy, i)
+        return remote(
+            passing.at[4 * side + i], slot(dy, h, 1, k), pass_ss.at[4 * side + i], w_rs.at[dy, h, 1, k], xn
+        )
+
+    def onward_copy(i):
+        h = quarter(dy_own, i)
+        return remote(passing.at[i], slot(dy_own, h, 0, k), pass_ss.at[i], w_rs.at[dy_own, h, 0, k], xn)
 
     halo_f = remote(
         feats.at[:, pl.ds(ROWS - HALO, HALO)], fbuf.at[:, pl.ds(0, HALO)], halo_ss.at[0], halo_rs.at[0], nxt
@@ -85,15 +354,15 @@
 
     @pl.when(role == 0)
     def _():
-        for h in (0, 2, 1, 3):
+        for i in range(4):
+            h = quarter(dy_own, i)
             pltpu.make_async_copy(w_piece(h), slot(dy_own, h, 0, k), w_rs.at[dy_own, h, 0, k]).start()
-            x_copy(h, 0, x2, 0).start()
 
     @pl.when(role == 1)
     def _():
-        for h in (0, 2, 1, 3):
-            x_copy(h, 1, xp, 0).start()
-            x_copy(h, 1, xn, 1).start()
+        for i in range(4):
+            z_pass_copy(i, 0).start()
+            z_pass_copy(i, 1).start()
 
     def sib_copy(dy, h, r):
         here = slot(dy, h, r, k)
@@ -113,57 +382,146 @@
 
     kind_here = (z // 2 + y) % 2
     kind_below = (((z + 3) % 4) // 2 + y) % 2
-
-    def spread(lo, hi):
+    first_odd = 1 + 2 * ((((y + 1) % 4) // 2 + xh) % 2)
+
+    def unit_of(kind, u):
+        dy0, i0 = 2 - 2 * (u // 4), u % 4
+        odd = u % 2
+        dy1, i1 = first_odd * (1 - odd) + (4 - first_odd) * odd, u // 2
+        dy, i = dy0 + kind * (dy1 - dy0), i0 + kind * (i1 - i0)
+        return dy, quarter(dy, i)
+
+    def side_of(dy):
+        return (((y + dy) % 4) // 2 + xh) % 2
+
+    def piece_of(kind, n):
+        dy, h = unit_of(kind, n // 2)
+        return dy, h, (n + side_of(dy)) % 2
+
+    near_far = [(0, 0), (1, 0), (0, 1), (1, 1), (0, 2), (1, 2), (0, 3), (1, 3)]
+    near_far += [(t, i) for i in range(4) for t in (3, 2)]
+    far_far = [(0, 0), (1, 0), (3, 0), (2, 0), (0, 1), (3, 1), (2, 1), (1, 1)]
+    far_far += [(3, 2), (2, 2), (0, 2), (3, 3), (2, 3), (1, 2), (0, 3), (1, 3)]
+    mixed = [(t, i) for i in range(4) for t in (0, 1, 3, 2)]
+    far_side = side_of(2)
+    kind = kind_here + role * (kind_below - kind_here)
+    cls = role * 4 + kind * 2 + far_side
+
+    def pick(values):
+        a, b, c2, d = values
+        if a == b == c2 == d:
+            return a
+        return a + far_side * (b - a) + kind * (c2 - a) + kind * far_side * (d - c2 - b + a)
+
+    def pick_any(values):
+        if all(v == values[0] for v in values):
+            return values[0]
+        picked = jnp.int32(values[0])
+        for n in range(1, 8):
+            picked = jnp.where(cls == n, jnp.int32(values[n]), picked)
+        return picked
+
+    def xp_step(n):
         @pl.when(role == 0)
         def _():
-            def body(u, _):
-                dy, h = unit_of(kind_here, u)
-                for r in range(2):
-                    w_wait(dy, h, r, k)
-                    zp_copy(dy, h, r).start()
-                    zm_copy(dy, h, r).start()
-                    sib_copy(dy, h, r).start()
-                return 0
-
-            lax.fori_loop(lo, hi, body, 0)
-
-    def relay(lo, hi):
-        @pl.when(role == 0)
-        def _():
-            def body(u, _):
-                dy, h = unit_of(1 - kind_here, u)
-                for r in range(2):
-                    w_wait(dy, h, r, k)
-                    sib_copy(dy, h, r).start()
-                return 0
-
-            lax.fori_loop(lo, hi, body, 0)
+            pass_copy(n).start()
 
         @pl.when(role == 1)
         def _():
-            def body(u, _):
-                dya, ha = unit_of(kind_below, u)
-                dyb, hb = unit_of(1 - kind_below, u)
-                for r in range(2):
-                    w_wait(dya, ha, r, k)
-                    if r == 0:
-                        zp_copy(dya, ha, r).start()
-                    sib_copy(dya, ha, r).start()
-                    w_wait(dyb, hb, r, k)
-                    if r == 1:
-                        zm_copy(dyb, hb, r).start()
-                    sib_copy(dyb, hb, r).start()
-                return 0
-
-            lax.fori_loop(lo, hi, body, 0)
+            x_copy(n, 0).start()
+
+    def z_onward_step(n):
+        for side in range(2):
+            z_pass_copy(n, side).wait_recv()
+            z_onward_copy(n, side).start()
+
+    def spread_step(n):
+        code = jnp.int32(0)
+        for m in range(16):
+            choices = [t * 4 + i for t, i in (near_far[m], far_far[m], mixed[m], mixed[m])]
+            code = jnp.where(n == m, pick(choices), code)
+        t, i = code // 4, code % 4
+        dy = (dy_own + 2 * (t // 2)) % 4
+        h, r = quarter(dy, i), t % 2
+        w_wait(dy, h, r, k)
+
+        @pl.when(t != 3)
+        def _():
+            zp_copy(dy, h, r).start()
+            zm_copy(dy, h, r).start()
+
+        sib_copy(dy, h, r).start()
+
+    def relay_step(n):
+        dy, h, r = piece_of(1 - kind_here, n)
+        w_wait(dy, h, r, k)
+        sib_copy(dy, h, r).start()
+
+    def xn_step(n):
+        i = n // 2
+
+        @pl.when(n % 2 == 0)
+        def _():
+            x_copy(i, 1).start()
+
+        @pl.when(n % 2 == 1)
+        def _():
+            pass_copy(i).wait_recv()
+            onward_copy(i).start()
+
+    def from_below_step(n):
+        dy, h, r = piece_of(kind_below, n)
+        w_wait(dy, h, r, k)
+
+        @pl.when(r == 0)
+        def _():
+            zp_copy(dy, h, r).start()
+
+        sib_copy(dy, h, r).start()
+
+    def from_above_step(n):
+        dy, h, r = piece_of(1 - kind_below, n)
+        w_wait(dy, h, r, k)
+
+        @pl.when(r == 1)
+        def _():
+            zm_copy(dy, h, r).start()
+
+        sib_copy(dy, h, r).start()
+
+    sequences = (
+        (xp_step, z_onward_step, spread_step, relay_step),
+        (xp_step, xn_step, from_below_step, from_above_step),
+    )
+
+    def transfers(point):
+        for r in range(2):
+            now = TRANSFERS[point][4 * r : 4 * r + 4]
+            then = TRANSFERS[point - 1][4 * r : 4 * r + 4] if point else ((0,) * 4,) * 4
+            if now == then:
+                continue
+
+            @pl.when(role == r)
+            def _():
+                for q, step in enumerate(sequences[r]):
+                    lo, hi = [v[q] for v in then], [v[q] for v in now]
+                    if lo != hi:
+                        def body(n, _, step=step):
+                            step(n)
+                            return 0
+
+                        lax.fori_loop(pick(lo), pick(hi), body, 0)
 
     def toep_body(g, _):
         row = jnp.broadcast_to(rtaps[pl.ds(g, 1)], (BLK, 2 * BLK))
         toep[g] = pltpu.roll(row, 1, 1, stride=1, stride_axis=0).astype(BF16)
         return 0
 
-    lax.fori_loop(0, CH // GROUP, toep_body, 0)
+    transfers(0)
+    lax.fori_loop(0, CH // GROUP // 2, toep_body, 0)
+    transfers(1)
+    lax.fori_loop(CH // GROUP // 2, CH // GROUP, toep_body, 0)
+    transfers(2)
 
     first = (c > 0).astype(F32)
 
@@ -195,28 +553,13 @@
 
         lax.fori_loop(0, CH // LANES, body, 0)
 
-    for cp in f_copies:
-        cp.wait()
-    gate(NB - 1)
-    halo_g = remote(gbuf.at[NB], gbuf.at[0], halo_ss.at[1], halo_rs.at[1], nxt)
-    halo_g.start()
-
-    def gate_body(i, _):
-        gate(NB - 2 - i)
-        return 0
-
-    lax.fori_loop(0, NB - 2, gate_body, 0)
-    halo_f.wait_recv()
-    gate(0)
-    spread(0, 4)
-
     def mix_copy(m):
         rows = pl.ds(m * CHUNK, CHUNK)
         return remote(mix.at[0, rows], mix.at[1, rows], mix_ss.at[m], mix_rs.at[m], xp)
 
     lane_group = lax.broadcasted_iota(jnp.int32, (BLK, 2 * LANES), 1) % LANES // GROUP
 
-    def mix_pair(b0):
+    def mix_pair(b0, lo, hi):
         keeps = [keep_of(b0), keep_of(b0 + 1)]
 
         def body(lt, _):
@@ -239,20 +582,38 @@
                 mix[0, pl.ds(pl.multiple_of((b0 + i) * BLK, BLK), BLK), lanes] = (query * direct).astype(BF16)
             return 0
 
-        lax.fori_loop(0, CH // LANES, body, 0)
+        lax.fori_loop(lo, hi, body, 0)
 
     chunk_at = [NCHUNK - 1 - i for i in range(NCHUNK)]
 
-    def chunk_body(i, _):
-        m = NCHUNK - 1 - i
-        mix_pair(2 * m)
+    tiles = CH // LANES
+    for cp in f_copies:
+        cp.wait()
+    gate(NB - 1)
+    halo_g = remote(gbuf.at[NB], gbuf.at[0], halo_ss.at[1], halo_rs.at[1], nxt)
+    halo_g.start()
+    transfers(3)
+    point = 4
+    for m in chunk_at:
+        if m > 0:
+            gate(2 * m)
+            gate(2 * m - 1)
+        else:
+            halo_f.wait_recv()
+            gate(0)
+            halo_g.wait_recv()
+        transfers(point)
+        point += 1
+        if m == NCHUNK - 1:
+            mix_pair(2 * m, 0, tiles // 2)
+            transfers(point)
+            point += 1
+            mix_pair(2 * m, tiles // 2, tiles)
+        else:
+            mix_pair(2 * m, 0, tiles)
         mix_copy(m).start()
-        return 0
-
-    lax.fori_loop(0, NCHUNK - 1, chunk_body, 0)
-    spread(4, 8)
-    halo_g.wait_recv()
-    chunk_body(NCHUNK - 1, 0)
+        transfers(point)
+        point += 1
 
     def rows_of(m):
         return pl.ds(pl.multiple_of(m * CHUNK, CHUNK), CHUNK)
@@ -266,7 +627,7 @@
         return dev(xh, z, k, (y + dy) % 4, xl)
 
     def far_copy(v, m):
-        dy, h = unit_of(0, v)
+        dy, h = 2, quarter(2, v)
         here = part.at[dy, h, rows_of(m)]
         return remote(here, got1.at[h, rows_of(m)], p_ss.at[dy, h, m], got1_rs.at[h, m], to_y(1 + 2 * (v % 2)))
 
@@ -284,49 +645,57 @@
         there = got2.at[side, h, rows_of(m)]
         remote(there, there, p_ss.at[0, h, m], got2_rs.at[side, h, m], yp).wait_recv()
 
-    def sib_wait(u):
-        for kind in range(2):
-            dy, h = unit_of(kind, u)
-            for r in range(2):
-                w_wait(dy, h, r, 1 - k)
-
-    for s in range(4):
-        relay(s, s + 1)
-        sib_wait(s)
-        mix_copy(chunk_at[s]).wait_recv()
-
-        def early_body(n, _):
-            u = jnp.minimum(n, s)
-            m = NCHUNK - 1 - jnp.where(n <= s, s, n - s - 1)
-            dy, h = unit_of(0, u)
-            part[dy, h, rows_of(m)] = project(dy, h, m).astype(BF16)
+    def tile_step(_, packed):
+        code = packed % 64
+        knd, u, m = code // 32, code // 4 % 8, code % 4
+        dy, h = unit_of(knd, u)
+        rows = rows_of(m)
+        total = project(dy, h, m)
+        depends = (knd == 1) & (u >= 4)
+
+        @pl.when(depends)
+        def _():
+            got1_wait(h, m)
+            part[dy, h, rows] = (total + got1[h, rows].astype(F32)).astype(BF16)
+
+        @pl.when(jnp.logical_not(depends))
+        def _():
+            part[dy, h, rows] = total.astype(BF16)
+
+        @pl.when((knd == 0) & (u < 4))
+        def _():
             far_copy(u, m).start()
-            dy, h = unit_of(1, u)
-            part[dy, h, rows_of(m)] = project(dy, h, m).astype(BF16)
+
+        @pl.when(knd == 1)
+        def _():
             near_copy(u, m).start()
-            return 0
-
-        lax.fori_loop(0, 2 * s + 1, early_body, 0)
-
-    def late_step(u, _):
-        relay(u, u + 1)
-        sib_wait(u)
-
-        def late_body(i, _):
-            m = NCHUNK - 1 - i
-            dy, h = unit_of(1, u)
-            got1_wait(h, m)
-            total = project(dy, h, m) + got1[h, rows_of(m)].astype(F32)
-            part[dy, h, rows_of(m)] = total.astype(BF16)
-            near_copy(u, m).start()
-            dy, h = unit_of(0, u)
-            part[dy, h, rows_of(m)] = project(dy, h, m).astype(BF16)
-            return 0
-
-        lax.fori_loop(0, NCHUNK, late_body, 0)
-        return 0
-
-    lax.fori_loop(4, 8, late_step, 0)
+
+        return packed // 64
+
+    chunks = [0] * 8
+    for p, phase in enumerate(PHASES):
+        if p:
+            transfers(point)
+            point += 1
+        for n, (waits, _, _) in enumerate(phase):
+            if waits:
+                @pl.when(cls == n)
+                def _():
+                    for code in waits:
+                        dy, h = unit_of(code // 8, code % 8)
+                        for r in range(2):
+                            w_wait(dy, h, r, 1 - k)
+
+        before = list(chunks)
+        chunks = [a + row[1] for a, row in zip(chunks, phase)]
+        if before != chunks:
+            def chunk_step(n, _):
+                mix_copy(NCHUNK - 1 - n).wait_recv()
+                return 0
+
+            lax.fori_loop(pick_any(before), pick_any(chunks), chunk_step, 0)
+        packed = [sum(code * 64**n for n, code in enumerate(row[2])) for row in phase]
+        lax.fori_loop(0, pick_any([len(row[2]) for row in phase]), tile_step, pick_any(packed) + jnp.int32(0))
 
     for h in (0, 2, 1, 3):
         def sum_body(i, _):
@@ -353,13 +722,6 @@
             for r in range(2):
                 sib_copy(dy, h, r).wait_send()
 
-        @pl.when(role == 0)
-        def _():
-            dy, h = unit_of(kind_here, u)
-            for r in range(2):
-                zp_copy(dy, h, r).wait_send()
-                zm_copy(dy, h, r).wait_send()
-
         @pl.when(role == 1)
         def _():
             dya, ha = unit_of(kind_below, u)
@@ -379,12 +741,21 @@
 
         @pl.when(role == 0)
         def _():
-            x_copy(v, 0, x2, 0).wait_send()
+            pass_copy(v).wait_send()
+            for t in range(3):
+                dy = (dy_own + 2 * (t // 2)) % 4
+                zp_copy(dy, quarter(dy, v), t % 2).wait_send()
+                zm_copy(dy, quarter(dy, v), t % 2).wait_send()
+            z_onward_copy(v, 0).wait_send()
+            z_onward_copy(v, 1).wait_send()
 
         @pl.when(role == 1)
         def _():
-            x_copy(v, 1, xp, 0).wait_send()
-            x_copy(v, 1, xn, 1).wait_send()
+            x_copy(v, 0).wait_send()
+            x_copy(v, 1).wait_send()
+            onward_copy(v).wait_send()
+            z_pass_copy(v, 0).wait_send()
+            z_pass_copy(v, 1).wait_send()
 
         return 0
 
@@ -403,6 +774,7 @@
         in_specs=[hbm, pl.BlockSpec(memory_space=pltpu.SMEM), vmem, vmem, vmem, hbm],
         out_specs=vmem,
         scratch_shapes=[
+            pltpu.VMEM((8, CH, LANES), BF16),
             pltpu.VMEM((3, HALO + ROWS, CH), BF16),
             pltpu.VMEM((3, 8 + BLK, CH), F32),
             pltpu.VMEM((NB + 1, BLK, CH), BF16),
@@ -417,6 +789,9 @@
             dma((3,)),
             dma((2,)),
             dma((2,)),
+            dma((8,)),
+            dma((8,)),
+            dma((4, 2)),
             dma((4, 4, 2, 2)),
             dma((4, 4, 2)),
             dma((4, 4, 2)),

time: 175 us -> 136 us (0.78)
  the two profiles are of different devices: /device:TPU:1 before, /device:TPU:16 now
where the time goes in v2:
time: 136 us
  Pallas kernels  132 us (97%)
  local copies, waits for them, and re-layouts  3.8 us (3%)
    pallas_call x1, Pallas kernels, on_device(): pl.pallas_call(kernel, out_shape=jax.ShapeDtypeStruct((ROWS, CH), BF16),...  132 us
    unnamed x1, local copies, waits for them, and re-layouts  3.08 us

profile of v2, /device:TPU:16, one launch (start us, length us, event | category | flops | bytes accessed | tf_op | source)
XLA Modules:
  0.0 136.3 jit_solution(4614686079749857378)
XLA Ops:
  0.0 0.8 convert_convert_fusion
  0.8 0.1 rev.3
  0.8 0.6 concatenate.3.rtaps
  1.5 131.7 %shard_map.64 = bf16[1024,1024]{1,0:T(8,128)(2,1)} custom-call(bf16[3,1024,1024]{2,1,0:T(8,128)(2,1)} %bitcast.3, s32[8]{0:T(128)} %starts.1, f32[3,7,1024]{2,1,0:T(8,128)} %bitcast.4, f32[64,256]{1,0:T(8,128)} %concatenate.3.rtaps, f32[1,1024]{1,0:T(1,128)} %bitcast.5, bf16[1024,512]{1,0:T(8,128)(2,1)} %w_ref.1), custom_call_target="tpu_custom_call" | custom-call | flops 17179869184 | bytes 16777216 | tf_op jit(solution)/shard_map/pallas_call | solution.py:771
  133.2 3.1 %copy.8 = bf16[1024,1024]{1,0:T(8,128)(2,1)} copy(bf16[1024,1024]{1,0:T(8,128)(2,1)} %shard_map.64) | data formatting | bytes 4194304

commit v3 on v2

--- a/solution.py
+++ b/solution.py
@@ -16,257 +16,268 @@
 SPAN = 7
 HALO = 16
 GROUP = 16
+OUT = jnp.bfloat16
 LANES = 128
 PER_TILE = LANES // GROUP
 CHUNK = 256
 NCHUNK = ROWS // CHUNK
 
 
+ORDERS = (
+    ((0, 4, 1, 5, 6, 2, 3, 7, 8, 14, 13, 9, 12, 10, 15, 11), (3, 1, 0, 2, 4, 5, 7, 6, 9, 10, 11, 8, 13, 12, 15, 14)),
+    ((0, 1, 12, 8, 4, 9, 5, 13, 14, 10, 2, 15, 11, 6, 3, 7), (0, 1, 3, 2, 4, 6, 5, 7, 10, 9, 8, 11, 14, 15, 12, 13)),
+    ((0, 4, 5, 12, 8, 1, 13, 9, 2, 14, 6, 10, 7, 15, 3, 11), (2, 0, 3, 1, 4, 5, 10, 7, 6, 8, 9, 11, 12, 13, 15, 14)),
+    ((0, 1, 4, 8, 13, 5, 12, 9, 2, 14, 6, 10, 15, 3, 7, 11), (1, 0, 2, 3, 4, 5, 6, 11, 8, 7, 12, 9, 15, 10, 14, 13)),
+    ((0, 2, 1, 3, 5, 10, 8, 4, 12, 6, 7, 9, 11, 14, 13, 15), (2, 1, 3, 0, 5, 6, 4, 7, 8, 9, 10, 11, 13, 14, 15, 12)),
+    ((0, 1, 9, 2, 3, 5, 4, 8, 6, 7, 10, 11, 12, 14, 13, 15), (0, 1, 2, 3, 5, 6, 7, 4, 9, 10, 8, 11, 14, 13, 15, 12)),
+    ((0, 2, 1, 3, 5, 6, 4, 7, 10, 8, 9, 11, 14, 13, 12, 15), (0, 1, 2, 3, 4, 5, 6, 10, 7, 8, 12, 9, 13, 11, 14, 15)),
+    ((0, 1, 3, 2, 4, 5, 7, 6, 8, 9, 11, 10, 12, 15, 13, 14), (1, 0, 2, 3, 4, 5, 10, 11, 6, 8, 7, 12, 9, 14, 15, 13)),
+)
 TRANSFERS = (
-    ((2, 0, 0, 0), (2, 0, 0, 0), (2, 0, 0, 0), (2, 0, 0, 0), (2, 1, 0, 0), (2, 1, 0, 0), (2, 1, 0, 0), (2, 1, 0, 0)),
-    ((2, 0, 1, 0), (2, 0, 1, 0), (2, 0, 1, 0), (2, 0, 1, 0), (2, 1, 0, 0), (2, 1, 0, 0), (2, 1, 0, 0), (2, 1, 0, 0)),
-    ((2, 0, 1, 0), (2, 0, 1, 0), (2, 0, 1, 0), (2, 0, 1, 0), (2, 1, 0, 0), (2, 1, 0, 0), (2, 1, 0, 0), (2, 1, 0, 0)),
-    ((2, 0, 1, 0), (2, 0, 1, 0), (2, 0, 1, 0), (2, 0, 1, 0), (2, 1, 0, 0), (2, 1, 0, 0), (2, 1, 0, 0), (2, 1, 0, 0)),
-    ((2, 1, 3, 0), (2, 1, 3, 0), (2, 1, 3, 0), (2, 1, 3, 0), (2, 3, 0, 0), (2, 3, 0, 0), (2, 3, 0, 0), (2, 3, 0, 0)),
-    ((2, 1, 3, 0), (2, 1, 3, 0), (2, 1, 3, 0), (2, 1, 3, 0), (2, 3, 1, 1), (2, 3, 0, 1), (2, 3, 1, 1), (2, 3, 1, 0)),
-    ((3, 1, 3, 0), (3, 1, 3, 0), (3, 1, 3, 0), (3, 1, 3, 0), (3, 3, 1, 1), (3, 3, 0, 1), (3, 3, 1, 1), (3, 3, 1, 0)),
-    ((3, 2, 5, 0), (3, 2, 5, 0), (3, 2, 6, 0), (3, 2, 6, 0), (3, 5, 1, 1), (3, 5, 0, 1), (3, 5, 1, 1), (3, 5, 1, 0)),
-    ((4, 2, 5, 0), (4, 2, 5, 0), (4, 2, 6, 0), (4, 2, 6, 0), (4, 5, 2, 2), (4, 5, 1, 2), (4, 5, 3, 2), (4, 5, 3, 0)),
-    ((4, 3, 5, 0), (4, 3, 5, 0), (4, 3, 6, 0), (4, 3, 6, 0), (4, 5, 2, 2), (4, 5, 1, 2), (4, 5, 3, 2), (4, 5, 3, 0)),
-    ((4, 3, 5, 0), (4, 3, 6, 0), (4, 3, 7, 0), (4, 3, 7, 0), (4, 5, 3, 4), (4, 5, 2, 4), (4, 5, 4, 3), (4, 5, 4, 2)),
-    ((4, 3, 5, 0), (4, 3, 6, 0), (4, 3, 7, 0), (4, 3, 7, 0), (4, 5, 3, 4), (4, 5, 2, 4), (4, 5, 4, 3), (4, 5, 4, 2)),
-    ((4, 4, 5, 0), (4, 4, 6, 0), (4, 4, 7, 0), (4, 4, 7, 0), (4, 5, 3, 4), (4, 5, 2, 4), (4, 5, 4, 3), (4, 5, 4, 2)),
-    ((4, 4, 6, 2), (4, 4, 8, 0), (4, 4, 9, 0), (4, 4, 9, 0), (4, 5, 4, 5), (4, 5, 4, 4), (4, 5, 5, 4), (4, 5, 6, 2)),
-    ((4, 4, 7, 4), (4, 4, 8, 4), (4, 4, 10, 2), (4, 4, 10, 2), (4, 7, 6, 6), (4, 7, 4, 8), (4, 7, 6, 6), (4, 7, 8, 4)),
-    ((4, 4, 7, 6), (4, 4, 11, 4), (4, 4, 12, 4), (4, 4, 12, 4), (4, 7, 6, 8), (4, 7, 5, 8), (4, 7, 8, 6), (4, 7, 8, 4)),
-    ((4, 4, 14, 6), (4, 4, 12, 6), (4, 4, 13, 4), (4, 4, 13, 4), (4, 7, 7, 9), (4, 7, 6, 9), (4, 7, 9, 7), (4, 7, 9, 6)),
-    ((4, 4, 15, 8), (4, 4, 12, 6), (4, 4, 13, 6), (4, 4, 13, 4), (4, 8, 7, 10), (4, 8, 6, 10), (4, 8, 10, 7), (4, 8, 10, 6)),
-    ((4, 4, 15, 8), (4, 4, 12, 8), (4, 4, 15, 6), (4, 4, 15, 6), (4, 8, 8, 11), (4, 8, 7, 12), (4, 8, 11, 8), (4, 8, 12, 6)),
-    ((4, 4, 15, 9), (4, 4, 13, 8), (4, 4, 15, 6), (4, 4, 16, 6), (4, 8, 9, 12), (4, 8, 7, 12), (4, 8, 12, 9), (4, 8, 12, 7)),
-    ((4, 4, 16, 9), (4, 4, 16, 10), (4, 4, 16, 7), (4, 4, 16, 6), (4, 8, 11, 12), (4, 8, 13, 13), (4, 8, 12, 11), (4, 8, 13, 13)),
-    ((4, 4, 16, 10), (4, 4, 16, 10), (4, 4, 16, 7), (4, 4, 16, 7), (4, 8, 11, 13), (4, 8, 13, 13), (4, 8, 13, 11), (4, 8, 13, 13)),
-    ((4, 4, 16, 10), (4, 4, 16, 10), (4, 4, 16, 8), (4, 4, 16, 8), (4, 8, 11, 13), (4, 8, 13, 13), (4, 8, 13, 11), (4, 8, 13, 13)),
-    ((4, 4, 16, 10), (4, 4, 16, 10), (4, 4, 16, 10), (4, 4, 16, 8), (4, 8, 13, 13), (4, 8, 13, 13), (4, 8, 13, 13), (4, 8, 15, 14)),
-    ((4, 4, 16, 10), (4, 4, 16, 12), (4, 4, 16, 10), (4, 4, 16, 10), (4, 8, 13, 15), (4, 8, 14, 15), (4, 8, 15, 13), (4, 8, 15, 14)),
-    ((4, 4, 16, 12), (4, 4, 16, 12), (4, 4, 16, 12), (4, 4, 16, 10), (4, 8, 15, 16), (4, 8, 15, 16), (4, 8, 16, 15), (4, 8, 15, 14)),
-    ((4, 4, 16, 12), (4, 4, 16, 12), (4, 4, 16, 12), (4, 4, 16, 12), (4, 8, 15, 16), (4, 8, 15, 16), (4, 8, 16, 15), (4, 8, 16, 15)),
-    ((4, 4, 16, 12), (4, 4, 16, 13), (4, 4, 16, 14), (4, 4, 16, 12), (4, 8, 15, 16), (4, 8, 15, 16), (4, 8, 16, 15), (4, 8, 16, 15)),
-    ((4, 4, 16, 13), (4, 4, 16, 13), (4, 4, 16, 16), (4, 4, 16, 14), (4, 8, 16, 16), (4, 8, 16, 16), (4, 8, 16, 16), (4, 8, 16, 16)),
-    ((4, 4, 16, 14), (4, 4, 16, 14), (4, 4, 16, 16), (4, 4, 16, 16), (4, 8, 16, 16), (4, 8, 16, 16), (4, 8, 16, 16), (4, 8, 16, 16)),
-    ((4, 4, 16, 14), (4, 4, 16, 14), (4, 4, 16, 16), (4, 4, 16, 16), (4, 8, 16, 16), (4, 8, 16, 16), (4, 8, 16, 16), (4, 8, 16, 16)),
-    ((4, 4, 16, 16), (4, 4, 16, 16), (4, 4, 16, 16), (4, 4, 16, 16), (4, 8, 16, 16), (4, 8, 16, 16), (4, 8, 16, 16), (4, 8, 16, 16)),
-    ((4, 4, 16, 16), (4, 4, 16, 16), (4, 4, 16, 16), (4, 4, 16, 16), (4, 8, 16, 16), (4, 8, 16, 16), (4, 8, 16, 16), (4, 8, 16, 16)),
+    ((1, 0, 0, 0), (1, 0, 0, 0), (2, 0, 1, 0), (2, 0, 0, 0), (1, 1, 1, 0, 0), (2, 1, 0, 0, 0), (1, 2, 1, 0, 0), (2, 1, 0, 0, 0)),
+    ((2, 0, 1, 0), (1, 0, 0, 0), (2, 0, 1, 0), (3, 0, 1, 0), (1, 1, 1, 0, 0), (2, 1, 0, 0, 0), (1, 3, 1, 0, 0), (2, 2, 0, 0, 0)),
+    ((2, 0, 1, 0), (2, 0, 0, 0), (3, 0, 1, 0), (3, 0, 1, 0), (3, 2, 1, 0, 0), (2, 2, 0, 0, 0), (3, 3, 1, 0, 0), (2, 2, 0, 0, 0)),
+    ((2, 0, 1, 0), (3, 0, 1, 0), (3, 0, 1, 0), (3, 0, 2, 0), (3, 2, 1, 0, 0), (2, 2, 1, 0, 0), (3, 3, 3, 0, 0), (2, 2, 1, 0, 0)),
+    ((2, 0, 2, 0), (3, 1, 2, 0), (3, 1, 2, 0), (3, 0, 3, 0), (3, 2, 1, 0, 0), (2, 4, 2, 0, 0), (3, 3, 3, 0, 0), (3, 3, 2, 0, 0)),
+    ((2, 0, 3, 0), (3, 1, 2, 0), (3, 1, 3, 0), (3, 2, 4, 0), (3, 2, 3, 0, 0), (2, 4, 3, 0, 0), (3, 4, 3, 0, 0), (3, 4, 2, 0, 0)),
+    ((3, 1, 4, 0), (3, 1, 2, 0), (3, 2, 3, 0), (3, 2, 4, 0), (3, 2, 3, 0, 0), (3, 4, 3, 0, 1), (3, 4, 5, 0, 1), (3, 4, 2, 0, 0)),
+    ((3, 2, 4, 0), (3, 1, 3, 0), (3, 2, 4, 0), (3, 2, 4, 0), (3, 3, 3, 0, 0), (3, 4, 3, 0, 1), (3, 4, 5, 1, 1), (3, 4, 3, 0, 0)),
+    ((4, 2, 4, 0), (4, 1, 5, 0), (3, 3, 5, 0), (4, 2, 5, 0), (4, 4, 3, 0, 0), (4, 4, 3, 0, 1), (4, 4, 5, 2, 1), (4, 4, 3, 0, 0)),
+    ((4, 3, 4, 0), (4, 1, 5, 0), (4, 3, 5, 0), (4, 2, 6, 0), (4, 4, 4, 0, 0), (4, 4, 3, 0, 1), (4, 4, 5, 3, 1), (4, 4, 6, 1, 0)),
+    ((4, 3, 4, 0), (4, 3, 5, 0), (4, 3, 6, 0), (4, 3, 6, 0), (4, 4, 5, 0, 0), (4, 4, 3, 0, 3), (4, 4, 5, 3, 2), (4, 4, 7, 2, 2)),
+    ((4, 4, 6, 0), (4, 3, 6, 0), (4, 3, 7, 0), (4, 4, 7, 0), (4, 4, 5, 1, 2), (4, 4, 5, 1, 3), (4, 4, 5, 4, 4), (4, 4, 7, 2, 2)),
+    ((4, 4, 6, 0), (4, 3, 8, 0), (4, 4, 8, 0), (4, 4, 8, 0), (4, 4, 5, 4, 5), (4, 4, 5, 4, 5), (4, 4, 6, 5, 4), (4, 4, 7, 6, 3)),
+    ((4, 4, 7, 4), (4, 3, 8, 0), (4, 4, 9, 1), (4, 4, 8, 0), (4, 4, 5, 4, 5), (4, 4, 6, 5, 5), (4, 4, 6, 6, 4), (4, 4, 7, 6, 3)),
+    ((4, 4, 7, 4), (4, 3, 9, 4), (4, 4, 11, 4), (4, 4, 11, 2), (4, 4, 7, 8, 7), (4, 4, 7, 5, 8), (4, 4, 7, 8, 6), (4, 4, 7, 7, 4)),
+    ((4, 4, 7, 6), (4, 3, 10, 4), (4, 4, 12, 5), (4, 4, 12, 4), (4, 4, 7, 8, 7), (4, 4, 7, 5, 8), (4, 4, 7, 8, 6), (4, 4, 7, 9, 4)),
+    ((4, 4, 13, 8), (4, 3, 11, 4), (4, 4, 12, 5), (4, 4, 12, 4), (4, 4, 8, 8, 10), (4, 4, 8, 8, 11), (4, 4, 7, 9, 6), (4, 4, 8, 9, 6)),
+    ((4, 4, 13, 8), (4, 4, 11, 8), (4, 4, 15, 5), (4, 4, 15, 6), (4, 4, 8, 9, 11), (4, 4, 8, 9, 11), (4, 4, 8, 11, 8), (4, 4, 8, 10, 6)),
+    ((4, 4, 13, 8), (4, 4, 12, 8), (4, 4, 15, 6), (4, 4, 16, 6), (4, 4, 8, 11, 11), (4, 4, 8, 9, 12), (4, 4, 8, 11, 11), (4, 4, 8, 10, 8)),
+    ((4, 4, 13, 8), (4, 4, 15, 8), (4, 4, 15, 6), (4, 4, 16, 6), (4, 4, 8, 11, 11), (4, 4, 8, 11, 13), (4, 4, 8, 11, 11), (4, 4, 8, 11, 10)),
+    ((4, 4, 14, 8), (4, 4, 15, 8), (4, 4, 15, 7), (4, 4, 16, 10), (4, 4, 8, 12, 12), (4, 4, 8, 11, 14), (4, 4, 8, 13, 11), (4, 4, 8, 13, 12)),
+    ((4, 4, 16, 8), (4, 4, 15, 8), (4, 4, 16, 7), (4, 4, 16, 10), (4, 4, 8, 12, 13), (4, 4, 8, 12, 14), (4, 4, 8, 14, 11), (4, 4, 8, 13, 12)),
+    ((4, 4, 16, 9), (4, 4, 16, 10), (4, 4, 16, 9), (4, 4, 16, 12), (4, 4, 8, 13, 14), (4, 4, 8, 13, 14), (4, 4, 8, 15, 14), (4, 4, 8, 13, 13)),
+    ((4, 4, 16, 10), (4, 4, 16, 12), (4, 4, 16, 12), (4, 4, 16, 12), (4, 4, 8, 13, 14), (4, 4, 8, 13, 15), (4, 4, 8, 15, 14), (4, 4, 8, 14, 13)),
+    ((4, 4, 16, 10), (4, 4, 16, 12), (4, 4, 16, 13), (4, 4, 16, 12), (4, 4, 8, 13, 14), (4, 4, 8, 15, 15), (4, 4, 8, 15, 14), (4, 4, 8, 16, 13)),
+    ((4, 4, 16, 10), (4, 4, 16, 12), (4, 4, 16, 13), (4, 4, 16, 16), (4, 4, 8, 15, 14), (4, 4, 8, 15, 16), (4, 4, 8, 16, 14), (4, 4, 8, 16, 16)),
+    ((4, 4, 16, 13), (4, 4, 16, 12), (4, 4, 16, 14), (4, 4, 16, 16), (4, 4, 8, 15, 16), (4, 4, 8, 15, 16), (4, 4, 8, 16, 16), (4, 4, 8, 16, 16)),
+    ((4, 4, 16, 13), (4, 4, 16, 12), (4, 4, 16, 14), (4, 4, 16, 16), (4, 4, 8, 16, 16), (4, 4, 8, 16, 16), (4, 4, 8, 16, 16), (4, 4, 8, 16, 16)),
+    ((4, 4, 16, 14), (4, 4, 16, 12), (4, 4, 16, 14), (4, 4, 16, 16), (4, 4, 8, 16, 16), (4, 4, 8, 16, 16), (4, 4, 8, 16, 16), (4, 4, 8, 16, 16)),
+    ((4, 4, 16, 15), (4, 4, 16, 16), (4, 4, 16, 16), (4, 4, 16, 16), (4, 4, 8, 16, 16), (4, 4, 8, 16, 16), (4, 4, 8, 16, 16), (4, 4, 8, 16, 16)),
+    ((4, 4, 16, 16), (4, 4, 16, 16), (4, 4, 16, 16), (4, 4, 16, 16), (4, 4, 8, 16, 16), (4, 4, 8, 16, 16), (4, 4, 8, 16, 16), (4, 4, 8, 16, 16)),
+    ((4, 4, 16, 16), (4, 4, 16, 16), (4, 4, 16, 16), (4, 4, 16, 16), (4, 4, 8, 16, 16), (4, 4, 8, 16, 16), (4, 4, 8, 16, 16), (4, 4, 8, 16, 16)),
+    ((4, 4, 16, 16), (4, 4, 16, 16), (4, 4, 16, 16), (4, 4, 16, 16), (4, 4, 8, 16, 16), (4, 4, 8, 16, 16), (4, 4, 8, 16, 16), (4, 4, 8, 16, 16)),
 )
 PHASES = (
     (
+        ((1, 0, 2), 1, (7, 3, 11)),
         ((0, 1), 1, (3, 7)),
-        ((0, 4), 1, (3, 19)),
-        ((8, 9), 1, (35, 39)),
-        ((8, 9), 1, (35, 39)),
+        ((9, 10), 1, (39, 43)),
+        ((10, 9, 8), 1, (43, 39, 35)),
+        ((0, 9, 8), 1, (3, 39, 35)),
         ((0, 8), 1, (3, 35)),
-        ((0, 8), 1, (3, 35)),
-        ((0, 8), 1, (3, 35)),
-        ((0, 8), 1, (3, 35)),
-    ),
-    (
-        ((2, 8), 0, (11, 35)),
-        ((1, 5), 0, (7, 23)),
-        ((10, 11), 0, (43, 47)),
-        ((10, 11), 0, (43, 47)),
-        ((9, 1), 0, (39, 7)),
-        ((9, 1), 0, (39, 7)),
-        ((9, 1), 0, (39, 7)),
-        ((9, 10), 0, (39, 43)),
-    ),
-    (
-        ((9,), 1, (39, 2, 6, 10, 34)),
-        ((8, 9), 0, (35, 39)),
-        ((12, 0), 0, (51, 3)),
-        ((12, 0), 0, (51, 3)),
-        ((10, 2), 0, (43, 11)),
-        ((10, 11), 0, (43, 47)),
-        ((10, 2), 0, (43, 11)),
-        ((1, 11), 0, (7, 47)),
-    ),
-    (
-        ((10,), 0, (38, 43, 42)),
-        ((2,), 1, (11, 2, 18, 6, 22)),
-        ((1, 13), 0, (7, 55)),
-        ((13, 1), 0, (55, 7)),
-        ((11,), 1, (47, 2, 34, 38, 6)),
-        ((), 1, (2, 34, 38, 6, 42)),
-        ((11,), 1, (47, 2, 34, 38, 6)),
-        ((), 1, (2, 34, 38, 42, 6)),
-    ),
-    (
+        ((0, 1, 9, 8), 1, (3, 7, 39, 35)),
+        ((9, 8), 1, (39, 35)),
+    ),
+    (
+        ((8,), 0, (35,)),
+        ((), 0, ()),
+        ((8,), 0, (35,)),
+        ((11,), 0, (47,)),
+        ((1,), 0, (7,)),
+        ((1,), 0, (7,)),
+        ((), 0, ()),
+        ((0,), 0, (3,)),
+    ),
+    (
+        ((), 1, (6, 2)),
+        ((9, 8), 0, (39, 35)),
+        ((0, 1), 1, (3, 34, 6, 38)),
+        ((0, 12), 0, (3, 51)),
+        ((2, 10), 1, (34, 11, 42, 6)),
+        ((10, 9), 1, (43, 2, 38)),
+        ((10,), 0, (43,)),
+        ((10, 1), 1, (42, 2, 6)),
+    ),
+    (
+        ((10, 9), 0, (10, 43, 38)),
+        ((2,), 1, (2, 6, 10, 38)),
+        ((12, 13, 11), 0, (51, 55, 46, 47)),
+        ((1, 13), 1, (7, 38, 42, 55, 34)),
+        ((), 0, (2, 38, 43)),
+        ((11,), 0, (47, 6, 34, 46, 42)),
+        ((), 1, (6, 42, 34)),
+        ((11,), 0, (47, 38, 34, 46)),
+    ),
+    (
+        ((3,), 0, (15, 14, 42)),
+        ((5,), 0, (11, 34, 23)),
+        ((), 0, (7, 50, 2)),
+        ((), 0, (54, 50, 6, 2, 46)),
+        ((11,), 0, (46, 10, 47)),
+        ((2,), 0, (39, 10, 11)),
+        ((2, 11), 0, (2, 38, 10, 46)),
+        ((2,), 0, (11, 10, 7)),
+    ),
+    (
+        ((), 0, ()),
+        ((11, 10), 0, (47, 43, 22)),
+        ((14,), 0, (59,)),
+        ((2, 14), 1, (9, 59, 58, 5)),
+        ((12,), 0, (50, 51)),
+        ((12,), 0, (51, 50)),
+        ((12,), 0, (51, 50, 47, 11)),
+        ((12,), 0, (51, 50)),
+    ),
+    (
+        ((4, 5), 0, (18, 22, 39)),
+        ((4,), 0, (18, 46, 19, 42)),
+        ((2,), 0, (11, 54)),
+        ((), 0, (45, 37, 41, 10, 33)),
+        ((3,), 0, (15,)),
+        ((13,), 1, (55, 41, 1, 37, 5)),
+        ((3,), 1, (15, 33, 1, 13)),
+        ((), 1, (37, 1, 41, 33)),
+    ),
+    (
+        ((11,), 0, (46, 34, 19)),
         ((3,), 0, (15, 14)),
-        ((), 0, (34, 38, 10)),
-        ((), 1, (34, 38, 42, 46, 2)),
-        ((), 1, (34, 38, 42, 46, 2)),
-        ((), 0, (42, 10, 46)),
-        ((2,), 0, (46, 11, 10)),
-        ((), 0, (42, 10, 46)),
-        ((2,), 0, (46, 11, 10)),
-    ),
-    (
-        ((4,), 0, (19, 18)),
-        ((10,), 0, (43, 42)),
-        ((), 0, (6, 50)),
-        ((), 0, (6, 50, 54)),
-        ((12,), 0, (51, 50)),
-        ((12,), 0, (51, 50)),
-        ((12,), 0, (51, 50)),
-        ((12,), 0, (51, 50)),
-    ),
-    (
-        ((5,), 0, (23, 22)),
-        ((11,), 0, (47, 46)),
-        ((2,), 0, (11, 10, 54)),
-        ((2,), 0, (11, 10)),
-        ((3,), 0, (15, 14)),
-        ((13,), 0, (55, 54)),
-        ((3,), 0, (15, 14)),
-        ((13,), 0, (55, 54)),
-    ),
-    (
-        ((6,), 0, (27, 26)),
-        ((3,), 0, (15, 14)),
-        ((14,), 0, (59, 58)),
-        ((14,), 0, (59, 58)),
-        ((13,), 0, (55, 54)),
-        ((), 1, (1, 33, 37, 5, 41)),
-        ((13,), 0, (55, 54)),
-        ((), 1, (1, 33, 37, 41, 5)),
-    ),
-    (
-        ((11,), 0, (47, 46)),
-        ((6,), 0, (27, 26)),
-        ((15,), 1, (63, 33, 37, 41, 45)),
-        ((15,), 1, (63, 33, 37, 41, 45)),
-        ((), 1, (1, 33, 37, 5, 41)),
-        ((), 0, (45, 9)),
-        ((), 1, (1, 33, 37, 5, 41)),
-        ((), 0, (45, 9)),
-    ),
-    (
-        ((7,), 0, (31, 30)),
-        ((7,), 0, (31, 30)),
-        ((), 0, (1, 5, 9, 62)),
-        ((), 0, (1, 5, 9, 62, 49)),
-        ((), 0, (9, 45, 13)),
-        ((3,), 0, (15, 14, 13)),
-        ((), 0, (9, 45, 13)),
-        ((3,), 0, (15, 14, 13)),
-    ),
-    (
-        ((12,), 0, (51, 50)),
-        ((12,), 0, (51, 50)),
-        ((3,), 0, (15, 14, 13, 53, 49)),
-        ((3,), 0, (15, 14, 13)),
-        ((4,), 0, (19, 18, 17)),
-        ((4,), 0, (19, 18, 17)),
-        ((4,), 0, (19, 18, 17)),
-        ((4,), 0, (19, 18, 17)),
-    ),
-    (
-        ((), 1, (1, 5, 9, 33, 37)),
-        ((), 1, (1, 17, 5, 21, 33)),
-        ((4,), 0, (57, 19, 18, 17)),
-        ((), 1, (32, 36, 40, 44, 0)),
-        ((5,), 0, (23, 22, 21)),
-        ((5,), 0, (23, 22, 21, 49, 53)),
-        ((5,), 0, (23, 22, 21)),
-        ((5,), 0, (23, 22, 21, 53, 49)),
-    ),
-    (
-        ((), 0, (41, 13, 17, 21, 25)),
-        ((), 0, (37, 9, 41, 45, 13)),
-        ((), 1, (32, 36, 40, 44, 0)),
-        ((), 0, (4, 8, 12, 53, 57)),
-        ((14,), 0, (59, 58, 53)),
-        ((6,), 0, (27, 26, 25)),
-        ((14,), 0, (59, 58, 53)),
-        ((14,), 0, (59, 58)),
-    ),
-    (
-        ((), 0, (45, 29)),
-        ((), 0, (25, 29)),
-        ((), 0, (4, 8, 12, 16, 61)),
-        ((4,), 0, (19, 18, 17, 16, 61)),
-        ((), 1, (0, 32, 36, 4, 40)),
-        ((14,), 0, (59, 58)),
-        ((), 1, (0, 32, 36, 4, 40)),
-        ((6,), 0, (27, 26, 25)),
-    ),
-    (
-        ((13,), 0, (55, 54)),
-        ((13,), 0, (55, 54)),
-        ((5,), 0, (23, 22, 21, 20)),
-        ((5,), 0, (48, 23, 22, 21, 20)),
-        ((), 0, (8, 44, 12, 16, 20)),
-        ((), 1, (0, 32, 36, 4, 40)),
-        ((), 0, (8, 44, 12, 16, 20)),
-        ((), 1, (0, 32, 36, 40, 4)),
-    ),
-    (
-        ((), 1, (0, 4, 8, 32, 36)),
-        ((), 1, (0, 16, 4, 20, 32)),
-        ((6,), 0, (27, 26, 25, 24, 52)),
-        ((), 0, (52, 56)),
-        ((6,), 0, (49, 27, 26, 25, 24)),
-        ((), 0, (44, 8, 12, 16, 20)),
-        ((6,), 0, (49, 27, 26, 25, 24)),
-        ((), 0, (44, 8, 12, 16, 20)),
-    ),
-    (
-        ((), 0, (40, 12, 16, 20, 24)),
-        ((), 0, (36, 8, 40, 44, 12)),
-        ((7,), 0, (48, 31, 30, 29, 28)),
-        ((6,), 0, (27, 26, 25, 24, 60)),
-        ((15,), 0, (63, 62, 57, 61)),
-        ((), 0, (24, 57)),
-        ((15,), 0, (63, 62, 57, 61)),
-        ((), 0, (24, 57)),
-    ),
-    (
-        ((), 0, (44, 28, 53, 49)),
-        ((), 0, (24, 28, 49, 53)),
-        ((), 0, (56, 60)),
-        ((7,), 0, (31, 30, 29, 28)),
-        ((7,), 0, (31, 30, 29, 28, 48)),
-        ((15,), 0, (63, 62, 61)),
-        ((7,), 0, (31, 30, 29, 28, 48)),
-        ((15,), 0, (63, 62, 61)),
-    ),
-    (
-        ((14,), 0, (59, 58, 57)),
-        ((14,), 0, (59, 58, 57)),
+        ((), 1, (58, 10, 37)),
+        ((15,), 0, (1, 11, 63)),
+        ((), 1, (37, 1, 5)),
+        ((3,), 0, (33, 15)),
+        ((), 0, (5, 14, 41)),
+        ((), 0, (5, 9, 45)),
+    ),
+    (
+        ((), 1, (33, 9, 23, 5, 45)),
+        ((6,), 1, (33, 41, 9, 25, 1)),
+        ((), 0, (33, 45, 1)),
+        ((3,), 0, (14, 15, 53, 62, 57)),
+        ((4,), 0, (9, 41, 17, 45)),
+        ((), 0, (54,)),
+        ((13,), 0, (55,)),
+        ((5, 3, 13), 0, (23, 15, 54)),
+    ),
+    (
+        ((), 0, (13,)),
+        ((), 0, (37, 27, 5, 21, 17)),
+        ((15,), 0, (5, 41, 63)),
+        ((), 1, (32, 49, 40, 0)),
+        ((13,), 0, (14, 18, 55, 13)),
+        ((), 0, (14, 13)),
+        ((), 0, (45, 37, 9)),
+        ((), 1, (13, 14, 4, 44, 43)),
+    ),
+    (
+        ((6,), 0, (1, 47, 27, 26, 41)),
+        ((7,), 0, (45, 31, 13)),
+        ((3,), 1, (4, 42, 15, 57)),
+        ((4,), 0, (36, 16)),
+        ((), 0, (53, 49)),
+        ((4,), 1, (16, 8, 19, 4, 17)),
+        ((6,), 1, (8, 25, 32)),
+        ((), 0, (49,)),
+    ),
+    (
+        ((7,), 1, (0, 37, 30)),
+        ((12,), 1, (4, 50)),
+        ((5,), 0, (13, 36, 23)),
+        ((), 0, (13, 44, 4, 18)),
+        ((), 1, (44, 36, 19, 33, 32)),
+        ((), 0, (9, 45, 49)),
+        ((), 0, (4, 54)),
+        ((), 0, (55, 40, 21)),
+    ),
+    (
+        ((), 0, (21, 32, 31)),
+        ((), 0, (0, 40, 20)),
+        ((), 0, (9, 0, 21)),
+        ((), 0, (61, 12, 48, 8)),
+        ((), 0, (8, 12)),
+        ((6,), 0, (27, 0, 40)),
+        ((4,), 0, (18, 44, 53, 12, 19)),
+        ((14,), 0, (57, 22, 32, 0)),
+    ),
+    (
+        ((), 0, (44, 8, 4)),
+        ((13,), 0, (24, 54, 36)),
+        ((4,), 0, (17, 53, 8, 14)),
+        ((6, 5), 0, (25, 52, 20)),
+        ((6, 5), 0, (24, 16, 4, 23)),
+        ((15, 5), 0, (63, 21)),
+        ((5, 14), 0, (23, 59, 0, 22)),
+        ((15, 7), 0, (8, 61, 30, 58)),
+    ),
+    (
+        ((12,), 0, (51,)),
+        ((), 0, (26, 49)),
+        ((6,), 0, (20, 26, 12, 52)),
+        ((), 0, (24, 27, 56)),
+        ((14, 15), 0, (57, 61, 25, 21, 0)),
+        ((14,), 0, (61, 32, 59)),
+        ((15, 7), 0, (57, 61, 30, 17, 58)),
+        ((), 0, (62,)),
+    ),
+    (
+        ((13,), 0, (50, 55, 17, 49)),
+        ((), 0, (30, 12, 8, 55)),
+        ((), 0, (22, 16, 25, 49, 24)),
+        ((), 0, (19,)),
+        ((7,), 0, (20, 62, 58, 48, 28)),
+        ((), 0, (36, 62, 23)),
+        ((), 0, (31, 56, 29, 49)),
+        ((6,), 0, (31, 29, 59, 24, 20)),
+    ),
+    (
+        ((14,), 0, (12, 59, 54)),
+        ((), 0, (16, 32, 53, 44)),
+        ((), 0, (32, 62, 19)),
+        ((), 0, (26,)),
+        ((), 0, (54,)),
+        ((7,), 0, (12, 30, 57)),
+        ((), 0, (20, 62, 16, 27)),
+        ((4,), 0, (17, 12, 25, 52)),
+    ),
+    (
+        ((), 0, (36, 53, 57)),
+        ((15, 14), 0, (28, 62, 59, 57, 51)),
+        ((7,), 0, (61, 18, 40, 28)),
+        ((7,), 0, (28, 29, 17)),
+        ((), 0, (59, 56, 30)),
+        ((), 0, (18, 48, 58, 52, 24)),
+        ((), 0, (48, 26, 40)),
+        ((), 0, (16, 28)),
+    ),
+    (
+        ((15,), 0, (40, 20, 24, 25, 63)),
+        ((), 0, (58, 48, 56, 63, 52)),
+        ((), 0, (31, 48)),
+        ((), 0, (22,)),
+        ((), 0, (27, 52, 26)),
+        ((), 0, (56, 31, 20, 44)),
+        ((), 0, (52, 21, 36)),
+        ((), 0, (36, 18, 53)),
+    ),
+    (
+        ((), 0, (29, 48, 61, 58, 62)),
+        ((), 0, (29,)),
+        ((), 0, (44, 27)),
+        ((), 0, (21,)),
+        ((), 0, (22,)),
+        ((), 0, (28, 53, 26, 60, 25)),
         ((), 0, ()),
-        ((), 0, ()),
-        ((), 0, (52, 56, 60)),
-        ((7,), 0, (31, 30, 29, 28, 48)),
-        ((), 0, (52, 56, 60)),
-        ((7,), 0, (31, 30, 29, 28, 48)),
-    ),
-    (
-        ((15,), 0, (63, 62, 61, 52, 60)),
-        ((15,), 0, (63, 62, 61, 48, 52)),
-        ((), 0, ()),
-        ((), 0, ()),
-        ((), 0, ()),
-        ((), 0, (52, 56, 60)),
-        ((), 0, ()),
-        ((), 0, (52, 56, 60)),
-    ),
-    (
-        ((), 0, (48, 56)),
-        ((), 0, (56, 60)),
-        ((), 0, ()),
-        ((), 0, ()),
-        ((), 0, ()),
-        ((), 0, ()),
-        ((), 0, ()),
-        ((), 0, ()),
+        ((), 0, (26, 27, 63)),
+    ),
+    (
+        ((), 0, (28, 52, 16, 56, 60)),
+        ((), 0, (61, 60)),
+        ((), 0, (29, 60, 30, 56)),
+        ((), 0, (23, 30, 60, 31)),
+        ((), 0, (40, 63, 29, 60, 31)),
+        ((), 0, (22, 29)),
+        ((), 0, (63, 60, 28, 24)),
+        ((), 0, (48, 56, 60, 19)),
     ),
 )
 
@@ -277,10 +288,10 @@
 
 
 def kernel(
-    feats, starts, sw, rtaps, bias, w_ref, out_ref,
-    passing, fbuf, ext, gbuf, toep, xs, conv, mix, wts, part, got1, got2,
+    feats, starts, sw, taps, bias, w_ref, out_ref,
+    rtaps, passing, fbuf, ext, gbuf, toep, xs, conv, mix, wts, part, got1, got2, done,
     f_sem, halo_ss, halo_rs, pass_rs, pass_ss, zx_ss, w_rs, sib_ss, zp_ss, zm_ss, x_ss, mix_ss, mix_rs,
-    p_ss, got1_rs, got2_rs,
+    p_ss, got1_rs, got2_rs, out_sem,
 ):
     c, t = lax.axis_index("ctx"), lax.axis_index("tp")
     xh, z, k = c // 8, (c // 2) % 4, c % 2
@@ -358,12 +369,6 @@
             h = quarter(dy_own, i)
             pltpu.make_async_copy(w_piece(h), slot(dy_own, h, 0, k), w_rs.at[dy_own, h, 0, k]).start()
 
-    @pl.when(role == 1)
-    def _():
-        for i in range(4):
-            z_pass_copy(i, 0).start()
-            z_pass_copy(i, 1).start()
-
     def sib_copy(dy, h, r):
         here = slot(dy, h, r, k)
         return remote(here, here, sib_ss.at[dy, h, r], w_rs.at[dy, h, r, k], sib)
@@ -398,11 +403,6 @@
         dy, h = unit_of(kind, n // 2)
         return dy, h, (n + side_of(dy)) % 2
 
-    near_far = [(0, 0), (1, 0), (0, 1), (1, 1), (0, 2), (1, 2), (0, 3), (1, 3)]
-    near_far += [(t, i) for i in range(4) for t in (3, 2)]
-    far_far = [(0, 0), (1, 0), (3, 0), (2, 0), (0, 1), (3, 1), (2, 1), (1, 1)]
-    far_far += [(3, 2), (2, 2), (0, 2), (3, 3), (2, 3), (1, 2), (0, 3), (1, 3)]
-    mixed = [(t, i) for i in range(4) for t in (0, 1, 3, 2)]
     far_side = side_of(2)
     kind = kind_here + role * (kind_below - kind_here)
     cls = role * 4 + kind * 2 + far_side
@@ -430,16 +430,23 @@
         def _():
             x_copy(n, 0).start()
 
+    def z_pass_step(n):
+        z_pass_copy(n, 0).start()
+        z_pass_copy(n, 1).start()
+
     def z_onward_step(n):
         for side in range(2):
             z_pass_copy(n, side).wait_recv()
             z_onward_copy(n, side).start()
 
-    def spread_step(n):
+    def at(which, base, n):
         code = jnp.int32(0)
         for m in range(16):
-            choices = [t * 4 + i for t, i in (near_far[m], far_far[m], mixed[m], mixed[m])]
-            code = jnp.where(n == m, pick(choices), code)
+            code = jnp.where(n == m, pick([ORDERS[base + q][which][m] for q in range(4)]), code)
+        return code
+
+    def spread_step(n):
+        code = at(0, 0, n)
         t, i = code // 4, code % 4
         dy = (dy_own + 2 * (t // 2)) % 4
         h, r = quarter(dy, i), t % 2
@@ -453,7 +460,7 @@
         sib_copy(dy, h, r).start()
 
     def relay_step(n):
-        dy, h, r = piece_of(1 - kind_here, n)
+        dy, h, r = piece_of(1 - kind_here, at(1, 0, n))
         w_wait(dy, h, r, k)
         sib_copy(dy, h, r).start()
 
@@ -470,7 +477,7 @@
             onward_copy(i).start()
 
     def from_below_step(n):
-        dy, h, r = piece_of(kind_below, n)
+        dy, h, r = piece_of(kind_below, at(0, 4, n))
         w_wait(dy, h, r, k)
 
         @pl.when(r == 0)
@@ -480,7 +487,7 @@
         sib_copy(dy, h, r).start()
 
     def from_above_step(n):
-        dy, h, r = piece_of(1 - kind_below, n)
+        dy, h, r = piece_of(1 - kind_below, at(1, 4, n))
         w_wait(dy, h, r, k)
 
         @pl.when(r == 1)
@@ -491,13 +498,13 @@
 
     sequences = (
         (xp_step, z_onward_step, spread_step, relay_step),
-        (xp_step, xn_step, from_below_step, from_above_step),
+        (xp_step, z_pass_step, xn_step, from_below_step, from_above_step),
     )
 
     def transfers(point):
         for r in range(2):
             now = TRANSFERS[point][4 * r : 4 * r + 4]
-            then = TRANSFERS[point - 1][4 * r : 4 * r + 4] if point else ((0,) * 4,) * 4
+            then = TRANSFERS[point - 1][4 * r : 4 * r + 4] if point else ((0,) * 5,) * 4
             if now == then:
                 continue
 
@@ -511,6 +518,11 @@
                             return 0
 
                         lax.fori_loop(pick(lo), pick(hi), body, 0)
+
+    ends = lax.broadcasted_iota(jnp.int32, (BLK, BLK), 0) + lax.broadcasted_iota(jnp.int32, (BLK, BLK), 1)
+    mirror = (ends == BLK - 1).astype(F32).astype(BF16)
+    rtaps[:, pl.ds(0, BLK)] = jnp.dot(taps[...].astype(BF16), mirror, preferred_element_type=F32)
+    rtaps[:, pl.ds(BLK, BLK)] = jnp.zeros((CH // GROUP, BLK), F32)
 
     def toep_body(g, _):
         row = jnp.broadcast_to(rtaps[pl.ds(g, 1)], (BLK, 2 * BLK))
@@ -697,28 +709,14 @@
         packed = [sum(code * 64**n for n, code in enumerate(row[2])) for row in phase]
         lax.fori_loop(0, pick_any([len(row[2]) for row in phase]), tile_step, pick_any(packed) + jnp.int32(0))
 
-    for h in (0, 2, 1, 3):
-        def sum_body(i, _):
-            m = NCHUNK - 1 - i
-            rows = rows_of(m)
-            got2_wait(0, h, m)
-            got2_wait(1, h, m)
-            total = part[0, h, rows].astype(F32) + got2[0, h, rows].astype(F32) + got2[1, h, rows].astype(F32)
-            total = total.astype(BF16)
-            for core in range(2):
-                out_ref[rows, pl.ds(core * 512 + h * LANES, LANES)] = total[:, core * LANES : (core + 1) * LANES]
-            return 0
-
-        lax.fori_loop(0, NCHUNK, sum_body, 0)
-
     halo_f.wait_send()
     halo_g.wait_send()
     for m in range(NCHUNK):
         mix_copy(m).wait_send()
 
     def sent_body(u, _):
-        for kind in range(2):
-            dy, h = unit_of(kind, u)
+        for knd in range(2):
+            dy, h = unit_of(knd, u)
             for r in range(2):
                 sib_copy(dy, h, r).wait_send()
 
@@ -729,15 +727,14 @@
             zp_copy(dya, ha, 0).wait_send()
             zm_copy(dyb, hb, 1).wait_send()
 
-        for m in range(NCHUNK):
-            near_copy(u, m).wait_send()
         return 0
 
     lax.fori_loop(0, 8, sent_body, 0)
 
-    def far_sent_body(v, _):
+    def early_sent_body(v, _):
         for m in range(NCHUNK):
             far_copy(v, m).wait_send()
+            near_copy(v, m).wait_send()
 
         @pl.when(role == 0)
         def _():
@@ -759,21 +756,52 @@
 
         return 0
 
-    lax.fori_loop(0, 4, far_sent_body, 0)
+    lax.fori_loop(0, 4, early_sent_body, 0)
+
+    def out_copy(h, m):
+        rows = rows_of(m)
+        for core in range(2):
+            yield pltpu.make_async_copy(
+                done.at[h, rows, pl.ds(core * LANES, LANES)],
+                out_ref.at[rows, pl.ds(pl.multiple_of(core * 512 + h * LANES, LANES), LANES)],
+                out_sem.at[h, m, core],
+            )
+
+    def sum_body(n, _):
+        i, m = n // NCHUNK, NCHUNK - 1 - n % NCHUNK
+        h = 2 * (i % 2) + i // 2
+        rows = rows_of(m)
+        got2_wait(0, h, m)
+        got2_wait(1, h, m)
+        total = part[0, h, rows].astype(F32) + got2[0, h, rows].astype(F32) + got2[1, h, rows].astype(F32)
+        done[h, rows] = total.astype(done.dtype)
+        for cp in out_copy(h, m):
+            cp.start()
+        return 0
+
+    lax.fori_loop(0, 4 * NCHUNK, sum_body, 0)
+
+    def late_sent_body(u, _):
+        for m in range(NCHUNK):
+            near_copy(u, m).wait_send()
+            for cp in out_copy(u - 4, m):
+                cp.wait()
+        return 0
+
+    lax.fori_loop(4, 8, late_sent_body, 0)
 
 
 def on_device(features, contig_starts, short_filter, medium_filter, filter_bias, out_weight):
     vmem = pl.BlockSpec(memory_space=pltpu.VMEM)
     hbm = pl.BlockSpec(memory_space=pl.ANY)
     dma = pltpu.SemaphoreType.DMA
-    taps = medium_filter.astype(BF16).astype(F32)[:, ::-1]
-    taps = jnp.concatenate([taps, jnp.zeros_like(taps)], axis=1)
     return pl.pallas_call(
         kernel,
-        out_shape=jax.ShapeDtypeStruct((ROWS, CH), BF16),
+        out_shape=jax.ShapeDtypeStruct((ROWS, CH), OUT),
         in_specs=[hbm, pl.BlockSpec(memory_space=pltpu.SMEM), vmem, vmem, vmem, hbm],
-        out_specs=vmem,
+        out_specs=hbm,
         scratch_shapes=[
+            pltpu.VMEM((CH // GROUP, 2 * BLK), F32),
             pltpu.VMEM((8, CH, LANES), BF16),
             pltpu.VMEM((3, HALO + ROWS, CH), BF16),
             pltpu.VMEM((3, 8 + BLK, CH), F32),
@@ -786,6 +814,7 @@
             pltpu.VMEM((4, 4, ROWS, 2 * LANES), BF16),
             pltpu.VMEM((4, ROWS, 2 * LANES), BF16),
             pltpu.VMEM((2, 4, ROWS, 2 * LANES), BF16),
+            pltpu.VMEM((4, ROWS, 2 * LANES), OUT),
             dma((3,)),
             dma((2,)),
             dma((2,)),
@@ -802,6 +831,7 @@
             dma((4, 4, NCHUNK)),
             dma((4, NCHUNK)),
             dma((2, 4, NCHUNK)),
+            dma((4, NCHUNK, 2)),
         ],
         compiler_params=pltpu.CompilerParams(
             collective_id=0, has_side_effects=True, vmem_limit_bytes=60 * 1024 * 1024
@@ -813,7 +843,7 @@
         jnp.transpose(features, (1, 0, 2)),
         contig_starts,
         jnp.transpose(short_filter, (1, 0, 2)),
-        taps,
+        medium_filter,
         filter_bias.reshape(1, CH),
         out_weight,
     )

time: 136 us -> 128 us (0.941); the launches traced: 136 us -> 126 us
  Pallas kernels: 132 us -> 123 us
    pallas_call x1, Pallas kernels: 132 us -> 123 us  [on_device(): pl.pallas_call(kernel, out_shape=jax.ShapeDtypeStruct((ROWS, CH), OUT), i...]
where the time goes in v3:
time: 128 us; the launch traced here: 126 us
  Pallas kernels  123 us (96%)
  local copies, waits for them, and re-layouts  3.08 us (2%)
    pallas_call x1, Pallas kernels, on_device(): pl.pallas_call(kernel, out_shape=jax.ShapeDtypeStruct((ROWS, CH), OUT), i...  123 us
    unnamed x1, local copies, waits for them, and re-layouts  3.08 us

profile of v3, /device:TPU:16, one launch (start us, length us, event | category | flops | bytes accessed | tf_op | source)
XLA Modules:
  0.0 125.7 jit_solution(10168750452249468164)
XLA Ops:
  0.0 122.6 %shard_map.64 = bf16[1024,1024]{1,0:T(8,128)(2,1)} custom-call(bf16[3,1024,1024]{2,1,0:T(8,128)(2,1)} %bitcast.3, s32[8]{0:T(128)} %starts.1, f32[3,7,1024]{2,1,0:T(8,128)} %bitcast.4, f32[64,128]{1,0:T(8,128)} %taps.1, f32[1,1024]{1,0:T(1,128)} %bitcast.5, bf16[1024,512]{1,0:T(8,128)(2,1)} %w_ref.1), custom_call_target="tpu_custom_call" | custom-call | flops 17179869184 | bytes 16777216 | tf_op jit(solution)/shard_map/pallas_call | solution.py:798
  122.6 3.1 %copy.8 = bf16[1024,1024]{1,0:T(8,128)(2,1)} copy(bf16[1024,1024]{1,0:T(8,128)(2,1)} %shard_map.64) | data formatting | bytes 4194304

commit v4 on v3

--- a/solution.py
+++ b/solution.py
@@ -779,16 +779,23 @@
             cp.start()
         return 0
 
-    lax.fori_loop(0, 4 * NCHUNK, sum_body, 0)
-
     def late_sent_body(u, _):
         for m in range(NCHUNK):
             near_copy(u, m).wait_send()
-            for cp in out_copy(u - 4, m):
+        return 0
+
+    def out_body(h, _):
+        for m in range(NCHUNK):
+            for cp in out_copy(h, m):
                 cp.wait()
         return 0
 
-    lax.fori_loop(4, 8, late_sent_body, 0)
+    lax.fori_loop(0, 3 * NCHUNK, sum_body, 0)
+    lax.fori_loop(0, 3, out_body, 0)
+    lax.fori_loop(4, 6, late_sent_body, 0)
+    lax.fori_loop(3 * NCHUNK, 4 * NCHUNK, sum_body, 0)
+    lax.fori_loop(6, 8, late_sent_body, 0)
+    out_body(3, 0)
 
 
 def on_device(features, contig_starts, short_filter, medium_filter, filter_bias, out_weight):

time: 128 us -> 128 us (level)
  no operation moved by 1% of the time
where the time goes in v4:
time: 128 us; the launch traced here: 126 us
  Pallas kernels  123 us (96%)
  local copies, waits for them, and re-layouts  3.08 us (2%)
    pallas_call x1, Pallas kernels, on_device(): pl.pallas_call(kernel, out_shape=jax.ShapeDtypeStruct((ROWS, CH), OUT), i...  123 us
    unnamed x1, local copies, waits for them, and re-layouts  3.08 us

profile of v4, /device:TPU:16, one launch (start us, length us, event | category | flops | bytes accessed | tf_op | source)
XLA Modules:
  0.0 125.7 jit_solution(8447678359152540987)
XLA Ops:
  0.0 122.6 %shard_map.64 = bf16[1024,1024]{1,0:T(8,128)(2,1)} custom-call(bf16[3,1024,1024]{2,1,0:T(8,128)(2,1)} %bitcast.3, s32[8]{0:T(128)} %starts.1, f32[3,7,1024]{2,1,0:T(8,128)} %bitcast.4, f32[64,128]{1,0:T(8,128)} %taps.1, f32[1,1024]{1,0:T(1,128)} %bitcast.5, bf16[1024,512]{1,0:T(8,128)(2,1)} %w_ref.1), custom_call_target="tpu_custom_call" | custom-call | flops 17179869184 | bytes 16777216 | tf_op jit(solution)/shard_map/pallas_call | solution.py:805
  122.6 3.1 %copy.8 = bf16[1024,1024]{1,0:T(8,128)(2,1)} copy(bf16[1024,1024]{1,0:T(8,128)(2,1)} %shard_map.64) | data formatting | bytes 4194304
